TPU v7x, 32 devices: a whole 2x2x4 slice. The times are simulated.
32 devices in a mesh: expert: 8 (over z, x), dp: 4 (over y, core).
Axes of the slice: x: 2, y: 2, z: 4, core: 2. Of those that a mesh axis runs over, the one named last changes fastest.
Arguments:
- tokens: bfloat16 [16384, 4096], P(('expert', 'dp')), may hold values from -6 to 6
- out_grad: bfloat16 [16384, 4096], P(('expert', 'dp')), may hold values from -6 to 6
- gates: bfloat16 [32, 1, 24], P(('expert', 'dp')), may hold values from 0.049804688 to 1
- picks: int32 [32, 1, 24], P(('expert', 'dp')), may hold values from 0 to 511, as said below
- counts: int32 [32, 1], P(('expert', 'dp')), may hold values from 1 to 24, as said below
- w_in: bfloat16 [8, 4096, 1024], P('expert'), may hold values from -0.09375 to 0.09375
- w_out: bfloat16 [8, 4096, 1024], P('expert'), may hold values from -0.0625 to 0.0625
Outputs:
- tokens_grad: bfloat16 [16384, 4096], P(('expert', 'dp'))
- gates_grad: float32 [32, 1, 24], P(('expert', 'dp'))
- w_in_grad: bfloat16 [8, 4096, 1024], P('expert', 'dp')
- w_out_grad: bfloat16 [8, 4096, 1024], P('expert', 'dp')
Inputs may be any that keep to these rules, and one draw needn't show every extreme that they name: picks[j, k, :] are 24 distinct rows of device j's tokens; slots at and beyond counts[j, k] hold rows too, but are not live. `counts`: in every draw some device fills all 24 slots of some expert.
All inputs are finite; a program needn't handle non-finite values.
Results may differ from a plain program's by a relative error of at most 0.013.
Values may be sent and summed in bfloat16 or wider, within the bound.
A program may use at most 192 MiB of HBM per device.

v0:
```python
import jax
import jax.numpy as jnp
from jax import lax
from jax.sharding import PartitionSpec as P

FF = 8192


def local(tokens, out_grad, gates, picks, counts, w_in, w_out):
    t_dev, model_width = tokens.shape
    expert_count = picks.shape[1]
    slot_count = picks.shape[2]
    part_units = w_in.shape[2]
    part_count = FF // part_units
    expert_devices = lax.axis_size("expert")
    row_index = picks[0].reshape(-1)
    picked_x = tokens[row_index].reshape(expert_count, slot_count, model_width)
    picked_dy = out_grad[row_index].reshape(expert_count, slot_count, model_width)
    live = jnp.arange(slot_count)[None, :] < counts[0][:, None]
    scale = jnp.where(live, gates[0], jnp.zeros_like(gates[0]))

    def spread(values):
        wide = jnp.broadcast_to(values[:, None], (expert_count, part_count) + values.shape[1:])
        return wide.reshape((expert_devices,) + values.shape[1:])

    got_x, got_dy, got_scale = (
        lax.all_to_all(spread(picked_x), "expert", split_axis=0, concat_axis=0, tiled=True),
        lax.all_to_all(spread(picked_dy), "expert", split_axis=0, concat_axis=0, tiled=True),
        lax.all_to_all(spread(scale), "expert", split_axis=0, concat_axis=0, tiled=True),
    )
    row_count = expert_devices * slot_count
    rows_x = got_x.reshape(row_count, model_width)
    rows_dy = got_dy.reshape(row_count, model_width)
    rows_scale = got_scale.reshape(row_count)
    scaled_dy = (rows_scale.astype(jnp.float32)[:, None] * rows_dy.astype(jnp.float32)).astype(
        jnp.bfloat16
    )
    weight_in = w_in[0]
    weight_out = w_out[0]
    pre = jnp.dot(rows_x, weight_in, preferred_element_type=jnp.float32)
    hidden, gelu_back = jax.vjp(jax.nn.gelu, pre)
    hidden = hidden.astype(jnp.bfloat16)
    part_out = lax.dot_general(
        hidden, weight_out, (((1,), (1,)), ((), ())), preferred_element_type=jnp.float32
    )
    gate_part = jnp.sum(rows_dy.astype(jnp.float32) * part_out, axis=-1)
    hidden_grad = jnp.dot(scaled_dy, weight_out, preferred_element_type=jnp.float32)
    pre_grad = gelu_back(hidden_grad)[0].astype(jnp.bfloat16)
    row_part = lax.dot_general(
        pre_grad, weight_in, (((1,), (1,)), ((), ())), preferred_element_type=jnp.float32
    )
    columns = rows_x
    w_in_grad = lax.psum_scatter(
        lax.dot_general(
            columns, pre_grad, (((0,), (0,)), ((), ())), preferred_element_type=jnp.float32
        ).astype(jnp.bfloat16),
        "dp",
        scatter_dimension=0,
        tiled=True,
    )[None]
    columns = scaled_dy
    w_out_grad = lax.psum_scatter(
        lax.dot_general(
            columns, hidden, (((0,), (0,)), ((), ())), preferred_element_type=jnp.float32
        ).astype(jnp.bfloat16),
        "dp",
        scatter_dimension=0,
        tiled=True,
    )[None]
    back_rows, back_gates = (
        lax.all_to_all(
            row_part.reshape(expert_devices, slot_count, model_width).astype(jnp.bfloat16),
            "expert",
            split_axis=0,
            concat_axis=0,
            tiled=True,
        ).astype(jnp.float32),
        lax.all_to_all(
            gate_part.reshape(expert_devices, slot_count).astype(jnp.bfloat16),
            "expert",
            split_axis=0,
            concat_axis=0,
            tiled=True,
        ).astype(jnp.float32),
    )
    summed_rows = jnp.sum(
        back_rows.reshape(expert_count, part_count, slot_count, model_width), axis=1
    )
    summed_gates = jnp.sum(back_gates.reshape(expert_count, part_count, slot_count), axis=1)
    empty_rows = jnp.zeros((t_dev, model_width), jnp.float32)
    tokens_grad = (
        empty_rows.at[row_index].add(summed_rows.reshape(-1, model_width)).astype(jnp.bfloat16)
    )
    gates_grad = jnp.where(live, summed_gates, jnp.zeros_like(summed_gates))[None]
    return (tokens_grad, gates_grad, w_in_grad, w_out_grad)


def solution(mesh):
    placed = (
        P(("expert", "dp"), None),
        P(("expert", "dp"), None),
        P(("expert", "dp"), None, None),
        P(("expert", "dp"), None, None),
        P(("expert", "dp"), None),
        P("expert", None, None),
        P("expert", None, None),
    )
    return jax.shard_map(
        local,
        mesh=mesh,
        in_specs=placed,
        out_specs=(
            P(("expert", "dp"), None),
            P(("expert", "dp"), None, None),
            P("expert", "dp", None),
            P("expert", "dp", None),
        ),
        check_vma=False,
    )
```

profile of v0, /device:TPU:0, one launch (start us, length us, event | category | flops | bytes accessed | tf_op | source)
XLA Modules:
  0.0 266.3 jit_solution(12714183434459738376)
XLA Ops:
  9.1 7.3 %all-to-all-start = ((bf16[8,1,24]{2,1,0:T(2,128)(2,1)}), bf16[8,1,24]{2,1,0:T(2,128)(2,1)S(1)}, u32[]{:S(2)}, u32[]{:S(2)}) async-start(bf16[8,1,24]{2,1,0:T(2,128)(2,1)} %reshape.141), calls=%async_computation | async-start | bytes 8192 | tf_op jit(solution)/shard_map/all_to_all | solution.py:29
  17.0 3.6 %gather_fusion.1 = bf16[24,4096]{1,0:T(8,128)(2,1)S(1)} fusion(bf16[512,4096]{1,0:T(8,128)(2,1)} %param.7, s32[1024]{0:T(1024)S(1)} %pad_clamp_fusion), kind=kCustom, calls=%fused_computation.1 | custom fusion | bytes 393312 | tf_op jit(solution)/shard_map/gather | solution.py:17
  20.6 2.1 all-to-all-done
  22.7 1.3 reshape.143
  24.0 3.9 %all-to-all-start.2 = ((bf16[8,24,4096]{2,1,0:T(8,128)(2,1)}), bf16[8,24,4096]{2,1,0:T(8,128)(2,1)S(1)}, u32[]{:S(2)}, u32[]{:S(2)}) async-start(bf16[8,24,4096]{2,1,0:T(8,128)(2,1)} %reshape.143), calls=%async_computation.2 | async-start | bytes 3145728 | tf_op jit(solution)/shard_map/all_to_all | solution.py:27
  27.9 3.6 %gather_fusion = bf16[24,4096]{1,0:T(8,128)(2,1)S(1)} fusion(bf16[512,4096]{1,0:T(8,128)(2,1)} %param.8, s32[1024]{0:T(1024)S(1)} %pad_clamp_fusion), kind=kCustom, calls=%fused_computation | custom fusion | bytes 393312 | tf_op jit(solution)/shard_map/gather | solution.py:18
  31.5 32.9 %all-to-all-done.2 = bf16[8,24,4096]{2,1,0:T(8,128)(2,1)S(1)} async-done(((bf16[8,24,4096]{2,1,0:T(8,128)(2,1)}), bf16[8,24,4096]{2,1,0:T(8,128)(2,1)S(1)}, u32[]{:S(2)}, u32[]{:S(2)}) %all-to-all-start.2) | async-done | bytes 1572896 | tf_op jit(solution)/shard_map/all_to_all | solution.py:27
  64.3 1.3 reshape.142
  65.7 3.6 %all-to-all-start.1 = ((bf16[8,24,4096]{2,1,0:T(8,128)(2,1)}), bf16[8,24,4096]{2,1,0:T(8,128)(2,1)S(1)}, u32[]{:S(2)}, u32[]{:S(2)}) async-start(bf16[8,24,4096]{2,1,0:T(8,128)(2,1)} %reshape.142), calls=%async_computation.1 | async-start | bytes 3145728 | tf_op jit(solution)/shard_map/all_to_all | solution.py:28
  69.4 6.1 %fusion.2 = f32[192,1024]{1,0:T(8,128)} fusion(bf16[192,4096]{1,0:T(8,128)(2,1)S(1)} %bitcast.45, bf16[1,4096,1024]{2,1,0:T(8,128)(2,1)} %param.12), kind=kOutput, calls=%fused_computation.5 | convolution fusion | flops 1610612736 | bytes 10747904 | tf_op jit(solution)/shard_map/dot_general | solution.py:40
  75.5 31.0 %all-to-all-done.1 = bf16[8,24,4096]{2,1,0:T(8,128)(2,1)S(1)} async-done(((bf16[8,24,4096]{2,1,0:T(8,128)(2,1)}), bf16[8,24,4096]{2,1,0:T(8,128)(2,1)S(1)}, u32[]{:S(2)}, u32[]{:S(2)}) %all-to-all-start.1) | async-done | bytes 1572896 | tf_op jit(solution)/shard_map/all_to_all | solution.py:28
  106.5 6.9 %convolution_convert_fusion = bf16[4096,1024]{1,0:T(8,128)(2,1)} fusion(f32[192]{0:T(256)S(1)} %reshape.147, f32[192,1024]{1,0:T(8,128)} %fusion.2, bf16[192,4096]{1,0:T(8,128)(2,1)S(1)} %bitcast.43), kind=kOutput, calls=%fused_computation.11 | convolution fusion | flops 1618935808 | bytes 10748672 | tf_op jit(solution)/shard_map/dot_general | solution.py:63
  114.0 0.7 copy-done
  114.8 5.8 %fusion.26 = bf16[192,1024]{1,0:T(8,128)(2,1)S(1)} fusion(f32[192,1024]{1,0:T(8,128)S(1)} %copy-done, bf16[192,4096]{1,0:T(8,128)(2,1)S(1)} %bitcast.47, bf16[1,4096,1024]{2,1,0:T(8,128)(2,1)} %param.13), kind=kOutput, calls=%fused_computation.30 | convolution fusion | flops 1614544896 | bytes 11141120 | tf_op jit(solution)/shard_map/dot_general | solution.py:47
  120.6 6.9 %convolution_convert_fusion.1 = bf16[4096,1024]{1,0:T(8,128)(2,1)} fusion(bf16[192,4096]{1,0:T(8,128)(2,1)S(1)} %bitcast.46, bf16[192,1024]{1,0:T(8,128)(2,1)S(1)} %fusion.26), kind=kOutput, calls=%fused_computation.12 | convolution fusion | flops 1614807040 | bytes 10354688 | tf_op jit(solution)/shard_map/dot_general | solution.py:54
  127.5 1.2 copy-done.1
  128.6 6.4 %fusion.17 = bf16[192]{0:T(256)(128)(2,1)S(1)} fusion(bf16[1,4096,1024]{2,1,0:T(8,128)(2,1)} %param.13, f32[192,1024]{1,0:T(8,128)S(1)} %copy-done.1, bf16[192,4096]{1,0:T(8,128)(2,1)S(1)} %bitcast.44), kind=kOutput, calls=%fused_computation.21 | convolution fusion | flops 1614741248 | bytes 10748288 | tf_op jit(solution)/shard_map/dot_general | solution.py:43
  135.8 4.4 %all-to-all-start.4 = ((bf16[8,1,24]{2,1,0:T(2,128)(2,1)}), bf16[8,1,24]{2,1,0:T(2,128)(2,1)S(1)}, u32[]{:S(2)}, u32[]{:S(2)}) async-start(bf16[8,1,24]{2,1,0:T(2,128)(2,1)} %convert_element_type.102), calls=%async_computation.4 | async-start | bytes 8192 | tf_op jit(solution)/shard_map/all_to_all | solution.py:78
  140.1 7.4 %fusion.11 = bf16[8,24,4096]{2,1,0:T(8,128)(2,1)} fusion(bf16[8,24,1024]{2,1,0:T(8,128)(2,1)S(1)} %bitcast.48, bf16[1,4096,1024]{2,1,0:T(8,128)(2,1)} %param.12), kind=kOutput, calls=%fused_computation.14 | convolution fusion | flops 1611399168 | bytes 10354688 | tf_op jit(solution)/shard_map/dot_general | solution.py:49
  147.5 6.0 %all-to-all-start.3 = ((bf16[8,24,4096]{2,1,0:T(8,128)(2,1)}), bf16[8,24,4096]{2,1,0:T(8,128)(2,1)S(1)}, u32[]{:S(2)}, u32[]{:S(2)}) async-start(bf16[8,24,4096]{2,1,0:T(8,128)(2,1)} %fusion.11), calls=%async_computation.3 | async-start | bytes 3145728 | tf_op jit(solution)/shard_map/all_to_all | solution.py:71
  154.1 36.1 %all-to-all-done.3 = bf16[8,24,4096]{2,1,0:T(8,128)(2,1)S(1)} async-done(((bf16[8,24,4096]{2,1,0:T(8,128)(2,1)}), bf16[8,24,4096]{2,1,0:T(8,128)(2,1)S(1)}, u32[]{:S(2)}, u32[]{:S(2)}) %all-to-all-start.3) | async-done | bytes 1572896 | tf_op jit(solution)/shard_map/all_to_all | solution.py:71
  190.4 5.9 %scatter_custom_fusion = f32[512,4096]{1,0:T(8,128)} fusion(s32[24]{0:T(128)S(1)} %fusion.30, f32[24,4096]{1,0:T(8,128)S(1)} %convert_reduce_fusion, f32[]{:T(128)} %constant.10.clone.1), kind=kCustom, calls=%fused_computation.15 | custom fusion | flops 98304 | bytes 8388612 | tf_op jit(solution)/shard_map/scatter-add | solution.py:92
  196.3 7.9 %convert_element_type.87 = bf16[512,4096]{1,0:T(8,128)(2,1)} convert(f32[512,4096]{1,0:T(8,128)} %scatter_custom_fusion) | non-fusion elementwise | flops 2097152 | bytes 12582912 | tf_op jit(solution)/shard_map/convert_element_type | solution.py:92
  204.2 55.3 %reduce-scatter.3.cloned.1.call-done = bf16[1024,1024]{1,0:T(8,128)(2,1)} async-done(((bf16[4096,1024]{1,0:T(8,128)(2,1)}), bf16[1024,1024]{1,0:T(8,128)(2,1)}) %reduce-scatter.3.cloned.1.call-update) | async-done | bytes 2097168 | tf_op jit(solution)/shard_map/reduce_scatter | solution.py:53
  (20 shorter events, 4.1 us)
Async XLA Ops:
  9.1 13.6 %all-to-all-start = ((bf16[8,1,24]{2,1,0:T(2,128)(2,1)}), bf16[8,1,24]{2,1,0:T(2,128)(2,1)S(1)}, u32[]{:S(2)}, u32[]{:S(2)}) async-start(bf16[8,1,24]{2,1,0:T(2,128)(2,1)} %reshape.141), calls=%async_computation | async-start | bytes 8192 | tf_op jit(solution)/shard_map/all_to_all | solution.py:29
  24.0 40.3 %all-to-all-start.2 = ((bf16[8,24,4096]{2,1,0:T(8,128)(2,1)}), bf16[8,24,4096]{2,1,0:T(8,128)(2,1)S(1)}, u32[]{:S(2)}, u32[]{:S(2)}) async-start(bf16[8,24,4096]{2,1,0:T(8,128)(2,1)} %reshape.143), calls=%async_computation.2 | async-start | bytes 3145728 | tf_op jit(solution)/shard_map/all_to_all | solution.py:27
  65.7 40.8 %all-to-all-start.1 = ((bf16[8,24,4096]{2,1,0:T(8,128)(2,1)}), bf16[8,24,4096]{2,1,0:T(8,128)(2,1)S(1)}, u32[]{:S(2)}, u32[]{:S(2)}) async-start(bf16[8,24,4096]{2,1,0:T(8,128)(2,1)} %reshape.142), calls=%async_computation.1 | async-start | bytes 3145728 | tf_op jit(solution)/shard_map/all_to_all | solution.py:28
  69.3 134.9 %reduce-scatter.5.cloned.1.call-start = ((), (), s32[]{:S(2)}) async-start(), calls=%async_computation.8 | async-start | bytes 10485760 | tf_op jit(solution)/shard_map/reduce_scatter | solution.py:62
  113.4 146.1 %reduce-scatter.3.cloned.1.call-start = ((), (), s32[]{:S(2)}) async-start(), calls=%async_computation.7 | async-start | bytes 10485760 | tf_op jit(solution)/shard_map/reduce_scatter | solution.py:53
  113.6 1.1 copy-start
  127.4 1.2 copy-start.1
  135.8 11.8 %all-to-all-start.4 = ((bf16[8,1,24]{2,1,0:T(2,128)(2,1)}), bf16[8,1,24]{2,1,0:T(2,128)(2,1)S(1)}, u32[]{:S(2)}, u32[]{:S(2)}) async-start(bf16[8,1,24]{2,1,0:T(2,128)(2,1)} %convert_element_type.102), calls=%async_computation.4 | async-start | bytes 8192 | tf_op jit(solution)/shard_map/all_to_all | solution.py:78
  147.5 42.7 %all-to-all-start.3 = ((bf16[8,24,4096]{2,1,0:T(8,128)(2,1)}), bf16[8,24,4096]{2,1,0:T(8,128)(2,1)S(1)}, u32[]{:S(2)}, u32[]{:S(2)}) async-start(bf16[8,24,4096]{2,1,0:T(8,128)(2,1)} %fusion.11), calls=%async_computation.3 | async-start | bytes 3145728 | tf_op jit(solution)/shard_map/all_to_all | solution.py:71
Sparse Core Ops, SparseCore 0:
  113.5 70.7 reduce-scatter.4
  187.7 71.7 reduce-scatter.2
where the time goes:
time: 267 us; the launch traced here: 266 us
  waiting for transfers between devices  157 us (59%)
  matrix products  39.4 us (15%)
  starting transfers between devices  25.4 us (10%)
  other arithmetic  16.3 us (6%)
  between operations  14.8 us (6%)
  local copies, waits for them, and re-layouts  13 us (5%)
    reduce_scatter x1, waiting for transfers between devices, local(): lax.psum_scatter(lax.dot_general(columns, pre_grad, (((0,), (0,)), ((), (...  55.3 us
    all_to_all x1, waiting for transfers between devices, local(): lax.all_to_all(row_part.reshape(expert_devices, slot_count, model_width)....  36.1 us
    all_to_all x1, waiting for transfers between devices, local(): lax.all_to_all(spread(picked_x), 'expert', split_axis=0, concat_axis=0, t...  32.9 us
    all_to_all x1, waiting for transfers between devices, local(): lax.all_to_all(spread(picked_dy), 'expert', split_axis=0, concat_axis=0,...  31 us
    convert_element_type x1, other arithmetic, local(): empty_rows.at[row_index].add(summed_rows.reshape(-1, model_width))  7.87 us
    dot_general x1, matrix products, local(): lax.dot_general(pre_grad, weight_in, (((1,), (1,)), ((), ())), preferred_...  7.38 us
    all_to_all x1, starting transfers between devices, local(): lax.all_to_all(spread(scale), 'expert', split_axis=0, concat_axis=0, tile...  7.25 us
    dot_general x1, matrix products, local(): lax.dot_general(columns, hidden, (((0,), (0,)), ((), ())), preferred_elem...  6.88 us
  transfers between devices with their start and end apart: 7, of which 5 were waited for; matrix products, arithmetic and copies ran while one was open for 21% of the time, Pallas kernels for 0%

commit v1 on v0

v1 whole, which is shorter than its diff:
```python
import functools

import jax
import jax.numpy as jnp
from jax import lax
from jax.experimental import pallas as pl
from jax.experimental.pallas import tpu as pltpu
from jax.sharding import PartitionSpec as P

FF = 8192
LANES = 128
MESH = pl.DeviceIdType.MESH


def meet(peers):
    barrier = pltpu.get_barrier_semaphore()
    for peer in peers:
        pl.semaphore_signal(barrier, inc=1, device_id=peer, device_id_type=MESH)
    pl.semaphore_wait(barrier, len(peers))


def send(src, dst, send_sem, recv_sem, peer):
    copy = pltpu.make_async_remote_copy(
        src_ref=src,
        dst_ref=dst,
        send_sem=send_sem,
        recv_sem=recv_sem,
        device_id=peer,
        device_id_type=MESH,
    )
    copy.start()
    return copy


def gather_kernel(
    width,
    own_x,
    own_dy,
    rows,
    slices,
    own_sem,
    z_send,
    z_recv,
    x_send,
    x_recv,
    dp_send,
    dp_recv,
    keep_sem,
):
    count = rows.shape[1]
    parts = slices.shape[1]
    lines = count // 2
    e = lax.axis_index("expert")
    d = lax.axis_index("dp")
    after = lax.rem(e + 2, count)
    before = lax.rem(e + count - 2, count)
    beside = e + 1 - 2 * lax.rem(e, 2)
    own = (
        pltpu.make_async_copy(own_x, rows.at[0, e], own_sem.at[0]),
        pltpu.make_async_copy(own_dy, rows.at[1, e], own_sem.at[1]),
    )
    for copy in own:
        copy.start()
    meet(
        [(after, d), (before, d), (beside, d)]
        + [(e, lax.rem(d + k, parts)) for k in range(1, parts)]
    )
    for copy in own:
        copy.wait()

    sent = []

    def block(b, c):
        return rows.at[:, b, :, pl.ds(c * width, width)]

    def to_z(b, s, c):
        sent.append(send(block(b, c), block(b, c), z_send.at[s, c], z_recv.at[s, c], (after, d)))

    def to_x(b, s, c):
        sent.append(send(block(b, c), block(b, c), x_send.at[s, c], x_recv.at[s, c], (beside, d)))

    def to_dp(b, c):
        @pl.when(d == c)
        def _():
            pltpu.make_async_copy(block(b, c), slices.at[:, d, b], keep_sem).start()

        @pl.when(d != c)
        def _():
            send(block(b, c), slices.at[:, d, b], dp_send, dp_recv.at[d], (e, c))

    def arrived(b, c, sem):
        pltpu.make_async_copy(block(b, c), block(b, c), sem).wait()

    for s in range(lines + 1):
        if s < lines:
            b = lax.rem(e + count - 2 * s, count)
            for c in range(parts):
                if s > 0:
                    arrived(b, c, z_recv.at[s - 1, c])
                if s < lines - 1:
                    to_z(b, s, c)
                to_x(b, s, c)
                to_dp(b, c)
        if s > 0:
            b = lax.rem(beside + count - 2 * (s - 1), count)
            for c in range(parts):
                arrived(b, c, x_recv.at[s - 1, c])
                to_dp(b, c)
    for copy in sent:
        copy.wait_send()
    out = slices.at[:, pl.ds(0, parts - 1)]
    pltpu.make_async_copy(out, out, dp_send).wait()
    kept = slices.at[:, d]
    pltpu.make_async_copy(kept, kept, keep_sem).wait()
    for k in range(1, parts):
        came = slices.at[:, lax.rem(d + k, parts)]
        pltpu.make_async_copy(came, came, dp_recv.at[lax.rem(d + k, parts)]).wait()


def gather_rows(own_x, own_dy, count, parts):
    slots, model_width = own_x.shape
    width = model_width // parts
    lines = count // 2
    dma = pltpu.SemaphoreType.DMA
    return pl.pallas_call(
        functools.partial(gather_kernel, width),
        out_shape=(
            jax.ShapeDtypeStruct((2, count, slots, model_width), jnp.bfloat16),
            jax.ShapeDtypeStruct((2, parts, count, slots, width), jnp.bfloat16),
        ),
        in_specs=[pl.BlockSpec(memory_space=pl.ANY)] * 2,
        out_specs=[pl.BlockSpec(memory_space=pl.ANY)] * 2,
        scratch_shapes=[
            dma((2,)),
            dma((lines - 1, parts)),
            dma((lines - 1, parts)),
            dma((lines, parts)),
            dma((lines, parts)),
            dma,
            dma((parts,)),
            dma,
        ],
        compiler_params=pltpu.CompilerParams(collective_id=0, has_side_effects=True),
        cost_estimate=pl.CostEstimate(flops=0, bytes_accessed=12 << 20, transcendentals=0),
        name="gather_rows",
    )(own_x, own_dy)


def return_kernel(
    spans,
    pre_grad,
    hidden,
    gate,
    weight,
    all_pre,
    all_hidden,
    rows_out,
    gates_out,
    w1,
    terms,
    beside_terms,
    pair_sum,
    line_terms,
    w_sem,
    own_sem,
    a_send,
    a_recv,
    x_send,
    x_recv,
    z_send,
    z_recv,
):
    parts = all_pre.shape[0]
    lines, slots = pair_sum.shape[0], pair_sum.shape[1]
    count = 2 * lines
    model_width = rows_out.shape[1]
    e = lax.axis_index("expert")
    d = lax.axis_index("dp")
    z = e // 2
    x = lax.rem(e, 2)
    beside = e + 1 - 2 * x
    twin = d + 1 - 2 * lax.rem(d, 2)
    across = lax.rem(d + 2, parts)
    load = pltpu.make_async_copy(weight, w1, w_sem)
    load.start()
    meet(
        [(beside, d), (e, twin), (e, across)]
        + [(lax.rem(e + 2 * t, count), d) for t in range(1, lines)]
    )
    sent = []
    pairs = ((pre_grad, all_pre), (hidden, all_hidden))
    for i, (src, dst) in enumerate(pairs):
        sent.append(send(src, dst.at[d], a_send.at[0, i], a_recv.at[0, i], (e, across)))
    for i, (src, dst) in enumerate(pairs):
        sent.append(send(src, dst.at[d], a_send.at[1, i], a_recv.at[1, i], (e, twin)))
        pltpu.make_async_copy(src, dst.at[d], own_sem.at[i]).start()

    def to_x(k):
        start, size = spans[k]
        cols = pl.ds(start, size)
        sent.append(
            send(
                terms.at[1 - x, :, :, cols],
                beside_terms.at[:, :, cols],
                x_send.at[k],
                x_recv.at[k],
                (beside, d),
            )
        )

    def keep(k, value):
        start, size = spans[k]
        value = value.reshape(lines, 2, slots, size).astype(jnp.bfloat16)
        terms[0, :, :, start : start + size] = value[:, 0]
        terms[1, :, :, start : start + size] = value[:, 1]

    keep(0, gate[...])
    to_x(0)
    load.wait()
    for k in range(1, len(spans)):
        start, size = spans[k]
        keep(
            k,
            lax.dot_general(
                pre_grad[...],
                w1[start : start + size, :],
                (((1,), (1,)), ((), ())),
                preferred_element_type=jnp.float32,
            ),
        )
        to_x(k)
    for k, (start, size) in enumerate(spans):
        cols = slice(start, start + size)
        here = pl.ds(start, size)
        pltpu.make_async_copy(
            beside_terms.at[:, :, here], beside_terms.at[:, :, here], x_recv.at[k]
        ).wait()
        pair_sum[:, :, cols] = (
            terms[x, :, :, cols].astype(jnp.float32)
            + beside_terms[:, :, cols].astype(jnp.float32)
        ).astype(jnp.bfloat16)
        for t in range(1, lines):
            sent.append(
                send(
                    pair_sum.at[lax.rem(z + t, lines), :, here],
                    line_terms.at[t - 1, :, here],
                    z_send.at[t - 1, k],
                    z_recv.at[t - 1, k],
                    (lax.rem(e + 2 * t, count), d),
                )
            )
    for i, (_, dst) in enumerate(pairs):
        came = dst.at[across]
        pltpu.make_async_copy(came, came, a_recv.at[0, i]).wait()
        sent.append(send(came, came, a_send.at[2, i], a_recv.at[2, i], (e, twin)))
    for k, (start, size) in enumerate(spans):
        cols = slice(start, start + size)
        here = pl.ds(start, size)
        total = terms[x, z, :, cols].astype(jnp.float32) + beside_terms[z, :, cols].astype(
            jnp.float32
        )
        for t in range(1, lines):
            came = line_terms.at[t - 1, :, here]
            pltpu.make_async_copy(came, came, z_recv.at[t - 1, k]).wait()
            total += line_terms[t - 1, :, cols].astype(jnp.float32)
        if start < model_width:
            rows_out[:, cols] = total.astype(jnp.bfloat16)
        else:
            gates_out[...] = total
    for i, (src, dst) in enumerate(pairs):
        pltpu.make_async_copy(src, dst.at[d], own_sem.at[i]).wait()
        for step, slot in ((1, twin), (2, lax.rem(twin + 2, parts))):
            came = dst.at[slot]
            pltpu.make_async_copy(came, came, a_recv.at[step, i]).wait()
    for copy in sent:
        copy.wait_send()


def return_rows(pre_grad, hidden, gate, weight, count, parts):
    row_count, units = pre_grad.shape
    slots = row_count // count
    lines = count // 2
    model_width = weight.shape[0]
    width = model_width // 4
    spans = [(model_width, LANES)] + [(k * width, width) for k in range(4)]
    wide = model_width + LANES
    dma = pltpu.SemaphoreType.DMA
    vmem = pl.BlockSpec(memory_space=pltpu.VMEM)
    anywhere = pl.BlockSpec(memory_space=pl.ANY)
    return pl.pallas_call(
        functools.partial(return_kernel, spans),
        out_shape=(
            jax.ShapeDtypeStruct((parts, row_count, units), jnp.bfloat16),
            jax.ShapeDtypeStruct((parts, row_count, units), jnp.bfloat16),
            jax.ShapeDtypeStruct((slots, model_width), jnp.bfloat16),
            jax.ShapeDtypeStruct((slots, LANES), jnp.float32),
        ),
        in_specs=[vmem, vmem, vmem, anywhere],
        out_specs=[anywhere, anywhere, vmem, vmem],
        scratch_shapes=[
            pltpu.VMEM((model_width, units), jnp.bfloat16),
            pltpu.VMEM((2, lines, slots, wide), jnp.bfloat16),
            pltpu.VMEM((lines, slots, wide), jnp.bfloat16),
            pltpu.VMEM((lines, slots, wide), jnp.bfloat16),
            pltpu.VMEM((lines - 1, slots, wide), jnp.bfloat16),
            dma,
            dma((2,)),
            dma((3, 2)),
            dma((3, 2)),
            dma((len(spans),)),
            dma((len(spans),)),
            dma((lines - 1, len(spans))),
            dma((lines - 1, len(spans))),
        ],
        compiler_params=pltpu.CompilerParams(
            collective_id=1, has_side_effects=True, vmem_limit_bytes=40 << 20
        ),
        cost_estimate=pl.CostEstimate(
            flops=2 * row_count * units * model_width,
            bytes_accessed=20 << 20,
            transcendentals=0,
        ),
        name="return_rows",
    )(pre_grad, hidden, gate, weight)


def local(tokens, out_grad, gates, picks, counts, w_in, w_out):
    t_dev, model_width = tokens.shape
    slot_count = picks.shape[2]
    parts = lax.axis_size("dp")
    count = lax.axis_size("expert")
    weight_in, weight_out = w_in[0], w_out[0]
    live = jnp.arange(slot_count)[None, :] < counts[0][:, None]
    scale = jnp.where(live, gates[0], jnp.zeros_like(gates[0]))
    chosen = picks[0, 0][:, None] == jnp.arange(t_dev)[None, :]
    chosen = chosen.astype(jnp.bfloat16)

    def pick(table):
        return jnp.dot(chosen, table, preferred_element_type=jnp.float32).astype(jnp.bfloat16)

    row_scale = lax.all_gather(scale[0], "expert", tiled=True).astype(jnp.float32)[:, None]
    rows, slices = gather_rows(pick(tokens), pick(out_grad), count, parts)
    row_count = count * slot_count
    pre = jnp.dot(
        rows[0].reshape(row_count, model_width), weight_in, preferred_element_type=jnp.float32
    )
    back = jnp.dot(
        rows[1].reshape(row_count, model_width), weight_out, preferred_element_type=jnp.float32
    )
    hidden, gelu_back = jax.vjp(jax.nn.gelu, pre)
    gate_part = jnp.sum(hidden * back, axis=-1, keepdims=True)
    gate_part = jnp.broadcast_to(gate_part, (row_count, LANES))
    pre_grad = gelu_back(row_scale * back)[0].astype(jnp.bfloat16)
    scaled_hidden = (row_scale * hidden).astype(jnp.bfloat16)
    all_pre, all_hidden, summed_rows, summed_gates = return_rows(
        pre_grad, scaled_hidden, gate_part, weight_in, count, parts
    )

    def weight_grad(columns, units):
        return lax.dot_general(
            columns.reshape(parts * row_count, model_width // parts),
            units.reshape(parts * row_count, units.shape[-1]),
            (((0,), (0,)), ((), ())),
            preferred_element_type=jnp.float32,
        ).astype(jnp.bfloat16)[None]

    tokens_grad = lax.dot_general(
        chosen, summed_rows, (((0,), (0,)), ((), ())), preferred_element_type=jnp.float32
    ).astype(jnp.bfloat16)
    gates_grad = jnp.where(live, summed_gates[:, 0][None], 0.0)[None]
    return (
        tokens_grad,
        gates_grad,
        weight_grad(slices[0], all_pre),
        weight_grad(slices[1], all_hidden),
    )


def local_many(tokens, out_grad, gates, picks, counts, w_in, w_out):
    t_dev, model_width = tokens.shape
    expert_count = picks.shape[1]
    slot_count = picks.shape[2]
    part_units = w_in.shape[2]
    part_count = FF // part_units
    expert_devices = lax.axis_size("expert")
    row_index = picks[0].reshape(-1)
    live = jnp.arange(slot_count)[None, :] < counts[0][:, None]
    scale = jnp.where(live, gates[0], jnp.zeros_like(gates[0]))

    def exchange(values):
        return lax.all_to_all(values, "expert", split_axis=0, concat_axis=0, tiled=True)

    def spread(values):
        wide = jnp.broadcast_to(values[:, None], (expert_count, part_count) + values.shape[1:])
        return exchange(wide.reshape((expert_devices,) + values.shape[1:]))

    row_count = expert_devices * slot_count
    picked_shape = (expert_count, slot_count, model_width)
    rows_x = spread(tokens[row_index].reshape(picked_shape)).reshape(row_count, model_width)
    rows_dy = spread(out_grad[row_index].reshape(picked_shape)).reshape(row_count, model_width)
    row_scale = spread(scale).reshape(row_count, 1).astype(jnp.float32)
    weight_in, weight_out = w_in[0], w_out[0]
    pre = jnp.dot(rows_x, weight_in, preferred_element_type=jnp.float32)
    back = jnp.dot(rows_dy, weight_out, preferred_element_type=jnp.float32)
    hidden, gelu_back = jax.vjp(jax.nn.gelu, pre)
    gate_part = jnp.sum(hidden * back, axis=-1)
    pre_grad = gelu_back(row_scale * back)[0].astype(jnp.bfloat16)
    scaled_hidden = (row_scale * hidden).astype(jnp.bfloat16)
    row_part = lax.dot_general(
        pre_grad, weight_in, (((1,), (1,)), ((), ())), preferred_element_type=jnp.float32
    )

    def weight_grad(columns, units):
        columns = lax.all_to_all(columns, "dp", split_axis=1, concat_axis=0, tiled=True)
        units = lax.all_gather(units, "dp", axis=0, tiled=True)
        return lax.dot_general(
            columns, units, (((0,), (0,)), ((), ())), preferred_element_type=jnp.float32
        ).astype(jnp.bfloat16)[None]

    back_shape = (expert_devices, slot_count, model_width)
    back_rows = exchange(row_part.reshape(back_shape).astype(jnp.bfloat16)).astype(jnp.float32)
    back_gates = exchange(gate_part.reshape(back_shape[:2]))
    summed_rows = jnp.sum(back_rows.reshape((expert_count, part_count) + back_shape[1:]), axis=1)
    summed_gates = jnp.sum(back_gates.reshape(expert_count, part_count, slot_count), axis=1)
    empty_rows = jnp.zeros((t_dev, model_width), jnp.float32)
    tokens_grad = (
        empty_rows.at[row_index].add(summed_rows.reshape(-1, model_width)).astype(jnp.bfloat16)
    )
    gates_grad = jnp.where(live, summed_gates, jnp.zeros_like(summed_gates))[None]
    return (
        tokens_grad,
        gates_grad,
        weight_grad(rows_x, pre_grad),
        weight_grad(rows_dy, scaled_hidden),
    )


def solution(mesh):
    placed = (
        P(("expert", "dp"), None),
        P(("expert", "dp"), None),
        P(("expert", "dp"), None, None),
        P(("expert", "dp"), None, None),
        P(("expert", "dp"), None),
        P("expert", None, None),
        P("expert", None, None),
    )

    def run(*arrays):
        one = arrays[3].shape[1] == 1 and mesh.shape["dp"] == 4
        return jax.shard_map(
            local if one else local_many,
            mesh=mesh,
            in_specs=placed,
            out_specs=(
                P(("expert", "dp"), None),
                P(("expert", "dp"), None, None),
                P("expert", "dp", None),
                P("expert", "dp", None),
            ),
            check_vma=False,
        )(*arrays)

    return run
```

time: 267 us -> 130 us (0.49)
  waiting for transfers between devices: 157 us -> 0 us
  Pallas kernels: 0 us -> 76.2 us
  starting transfers between devices: 25.4 us -> 0 us
  blocking collectives: 0 us -> 23.1 us
  matrix products: 39.4 us -> 22.7 us
  other arithmetic: 16.3 us -> 1.19 us
  between operations: 14.8 us -> 2.09 us
  local copies, waits for them, and re-layouts: 13 us -> 4.44 us
    all_to_all x5 -> x0, waiting for transfers between devices: 102 us -> none  [the longest x1 36.1 us: local(): lax.all_to_all(row_part.reshape(expert_devices, slot_count, model_width)....]
    pallas_call x0 -> x2, Pallas kernels: none -> 76.2 us  [the longest x1 46.4 us: gather_rows(): pl.pallas_call(functools.partial(gather_kernel, width), out_shape=(jax.Sh...]
    reduce_scatter x2 -> x0, waiting for transfers between devices: 55.3 us -> none  [the longest x1 55.3 us: local(): lax.psum_scatter(lax.dot_general(columns, pre_grad, (((0,), (0,)), ((), (...]
    all_to_all x5 -> x0, starting transfers between devices: 25.1 us -> none  [the longest x1 7.25 us: local(): lax.all_to_all(spread(scale), 'expert', split_axis=0, concat_axis=0, tile...]
    unnamed x0 -> x1, blocking collectives: none -> 23.1 us
    dot_general x6 -> x7, matrix products: 39.4 us -> 22.7 us  [the longest x2 6.32 us: weight_grad(): lax.dot_general(columns.reshape(parts * row_count, model_width // parts),...]
    convert_element_type x4 -> x1, other arithmetic: 8.27 us -> 0.01 us  [local(): lax.all_gather(scale[0], 'expert', tiled=True).astype(jnp.float32)[:, None]]
    gather x2 -> x0, local copies, waits for them, and re-layouts: 7.15 us -> none  [the longest x1 3.57 us: local(): picked_x = tokens[row_index].reshape(expert_count, slot_count, model_width)]
  transfers between devices with their start and end apart: 7 -> 0, of which waited for: 5 -> 0; matrix products, arithmetic and copies ran while one was open for 21% -> 0% of each run, Pallas kernels for 0% -> 0%
where the time goes in v1:
time: 130 us
  Pallas kernels  76.2 us (59%)
  blocking collectives  23.1 us (18%)
  matrix products  22.7 us (17%)
  local copies, waits for them, and re-layouts  4.44 us (3%)
  between operations  2.09 us (2%)
    pallas_call x1, Pallas kernels, gather_rows(): pl.pallas_call(functools.partial(gather_kernel, width), out_shape=(jax.Sh...  46.4 us
    pallas_call x1, Pallas kernels, return_rows(): pl.pallas_call(functools.partial(return_kernel, spans), out_shape=(jax.Sh...  29.8 us
    unnamed x1, blocking collectives  23.1 us
    dot_general x2, matrix products, weight_grad(): lax.dot_general(columns.reshape(parts * row_count, model_width // parts),...  6.32 us
    dot_general x1, matrix products, local(): jnp.dot(rows[0].reshape(row_count, model_width), weight_in, preferred_ele...  5.37 us
    dot_general x2, matrix products, pick(): jnp.dot(chosen, table, preferred_element_type=jnp.float32)  5.12 us
    dot_general x1, matrix products, local(): lax.dot_general(chosen, summed_rows, (((0,), (0,)), ((), ())), preferred_...  3.39 us

profile of v1, /device:TPU:0, one launch (start us, length us, event | category | flops | bytes accessed | tf_op | source)
XLA Modules:
  0.0 129.7 jit_solution(13378556296647268851)
XLA Ops:
  1.3 1.2 dynamic-slice
  3.2 0.7 compare_select_fusion.1
  3.8 0.2 dynamic-update-slice
  4.1 23.1 %all-reduce = bf16[192]{0:T(256)(128)(2,1)S(1)} all-reduce(bf16[192]{0:T(256)(128)(2,1)S(1)} %dynamic-update-slice), channel_id=1, replica_groups=mesh['expert'=8,'dp'=4] {'expert'}, use_global_device_ids=true, to_apply=%add | all-reduce | flops 192 | bytes 768
  27.2 0.0 copy-start.2
  27.2 3.7 %convolution_convert_fusion.2.own_x = bf16[24,4096]{1,0:T(8,128)(2,1)} fusion(bf16[512,4096]{1,0:T(8,128)(2,1)} %param.7, s32[24]{0:T(128)} %bitcast.45), kind=kOutput, calls=%fused_computation.4 | convolution fusion | flops 100773888 | bytes 4391008 | tf_op jit(solution)/shard_map/dot_general | solution.py:339
  30.9 0.0 copy-done.2
  30.9 1.4 %convolution_convert_fusion.1.own_dy = bf16[24,4096]{1,0:T(8,128)(2,1)} fusion(bf16[512,4096]{1,0:T(8,128)(2,1)S(1)} %copy-done, s32[24]{0:T(128)S(1)} %bitcast.46), kind=kOutput, calls=%fused_computation.3 | convolution fusion | flops 100773888 | bytes 4391008 | tf_op jit(solution)/shard_map/dot_general | solution.py:339
  32.3 46.4 %gather_rows.1 = (bf16[2,8,24,4096]{3,2,1,0:T(8,128)(2,1)}, bf16[2,4,8,24,1024]{4,3,2,1,0:T(8,128)(2,1)}) custom-call(bf16[24,4096]{1,0:T(8,128)(2,1)} %convolution_convert_fusion.2.own_x, bf16[24,4096]{1,0:T(8,128)(2,1)} %convolution_convert_fusion.1.own_dy), custom_call_target="tpu_custom_call" | custom-call | bytes 12582912 | tf_op jit(solution)/shard_map/gather_rows/pallas_call | solution.py:125
  78.7 0.0 slice-start.2
  78.7 2.4 %fusion.15 = (bf16[1,8,24,4096]{3,2,1,0:T(8,128)(2,1)S(1)}, bf16[1,8,24,4096]{3,2,1,0:T(8,128)(2,1)S(1)}) fusion(bf16[2,8,24,4096]{3,2,1,0:T(8,128)(2,1)} %get-tuple-element.10), kind=kLoop, calls=%fused_computation.29 | loop fusion | bytes 6291456 | tf_op jit(solution)/shard_map/slice | solution.py:348
  81.1 0.0 slice-start.3
  81.1 0.0 slice-start
  81.1 5.4 %fusion.12 = f32[192,1024]{1,0:T(8,128)S(1)} fusion(bf16[192,4096]{1,0:T(8,128)(2,1)S(1)} %bitcast.44, bf16[1,4096,1024]{2,1,0:T(8,128)(2,1)} %param.12), kind=kOutput, calls=%fused_computation.26 | convolution fusion | flops 1610612736 | bytes 10747904 | tf_op jit(solution)/shard_map/dot_general | solution.py:344
  86.6 0.0 slice-start.1
  86.6 2.5 %multiply_reduce_fusion = (f32[192]{0:T(256)S(1)}, bf16[192,1024]{1,0:T(8,128)(2,1)S(1)}, bf16[192,1024]{1,0:T(8,128)(2,1)S(1)}) fusion(f32[192,1024]{1,0:T(8,128)S(1)} %fusion.12, f32[192]{0:T(256)S(1)} %convert_element_type.25, bf16[192,4096]{1,0:T(8,128)(2,1)S(1)} %bitcast.41, bf16[1,4096,1024]{2,1,0:T(8,128)(2,1)S(1)} %bitcast.49), kind=kOutput, calls=%fused_computation.16 | convolution fusion | flops 1615724288 | bytes 11535872 | tf_op jit(solution)/shard_map/dot_general | solution.py:347
  89.1 0.1 broadcast_in_dim.10.gate
  89.2 29.8 %return_rows.1 = (bf16[4,192,1024]{2,1,0:T(8,128)(2,1)S(1)}, bf16[4,192,1024]{2,1,0:T(8,128)(2,1)S(1)}, bf16[24,4096]{1,0:T(8,128)(2,1)S(1)}, f32[24,128]{1,0:T(8,128)S(1)}) custom-call(bf16[192,1024]{1,0:T(8,128)(2,1)S(1)} %get-tuple-element.21.pre_grad, bf16[192,1024]{1,0:T(8,128)(2,1)S(1)} %get-tuple-element.22.hidden, ...), custom_call_target="tpu_custom_call" | custom-call | flops 1610612736 | bytes 20971520 | tf_op jit(solution)/shard_map/return_rows/pallas_call | solution.py:290
  119.0 0.1 slice_reduce_fusion
  119.1 0.5 compare_select_fusion
  119.6 0.4 fusion.14
  120.0 3.2 %convert_bitcast_fusion = bf16[1,1024,1024]{2,1,0:T(8,128)(2,1)} fusion(bf16[768,1024]{1,0:T(8,128)(2,1)S(1)} %bitcast.43, bf16[768,1024]{1,0:T(8,128)(2,1)S(1)} %bitcast.40), kind=kOutput, calls=%fused_computation.5 | convolution fusion | flops 1611661312 | bytes 5242880 | tf_op jit(solution)/shard_map/dot_general | solution.py:360
  123.2 3.2 %convert_bitcast_fusion.1 = bf16[1,1024,1024]{2,1,0:T(8,128)(2,1)} fusion(bf16[768,1024]{1,0:T(8,128)(2,1)S(1)} %bitcast.42, bf16[768,1024]{1,0:T(8,128)(2,1)S(1)} %bitcast.39), kind=kOutput, calls=%fused_computation.6 | convolution fusion | flops 1611661312 | bytes 5242880 | tf_op jit(solution)/shard_map/dot_general | solution.py:360
  126.3 3.4 %convolution_convert_fusion = bf16[512,4096]{1,0:T(8,128)(2,1)} fusion(bf16[24,4096]{1,0:T(8,128)(2,1)S(1)} %get-tuple-element.11, s32[24]{0:T(128)S(1)} %bitcast.47), kind=kOutput, calls=%fused_computation.2 | convolution fusion | flops 102772736 | bytes 4391008 | tf_op jit(solution)/shard_map/dot_general | solution.py:367
  (12 shorter events, 0.0 us)
Async XLA Ops:
  27.2 3.8 %copy-start = (bf16[512,4096]{1,0:T(8,128)(2,1)S(1)}, bf16[512,4096]{1,0:T(8,128)(2,1)}, u32[]{:S(2)}) copy-start(bf16[512,4096]{1,0:T(8,128)(2,1)} %param.8) | copy-start | bytes 12582916
  27.2 3.8 %copy-start.2 = (s32[1,1,24]{2,1,0:T(1,128)S(1)}, s32[1,1,24]{2,1,0:T(1,128)}, u32[]{:S(2)}) copy-start(s32[1,1,24]{2,1,0:T(1,128)} %param.10) | copy-start | bytes 292
  78.7 7.8 %slice-start.2 = ((s8[8388608]{0:T(1024)(128)(4,1)}), s8[4194304]{0:T(1024)(128)(4,1)S(1)}, s32[]{:S(2)}) async-start(s8[8388608]{0:T(1024)(128)(4,1)} %bitcast.48), calls=%async_computation.2 | async-start | bytes 8388608
  81.1 5.4 %slice-start.3 = ((s8[8388608]{0:T(1024)(128)(4,1)}), s8[4194304]{0:T(1024)(128)(4,1)S(1)}, s32[]{:S(2)}) async-start(s8[8388608]{0:T(1024)(128)(4,1)} %bitcast.48), calls=%async_computation.3 | async-start | bytes 8388608
  81.1 8.0 %slice-start = ((s8[8388608]{0:T(1024)(128)(4,1)}), s8[4194304]{0:T(1024)(128)(4,1)S(1)}, s32[]{:S(2)}) async-start(s8[8388608]{0:T(1024)(128)(4,1)} %bitcast.36), calls=%async_computation | async-start | bytes 8388608
  86.6 2.6 %slice-start.1 = ((s8[8388608]{0:T(1024)(128)(4,1)}), s8[4194304]{0:T(1024)(128)(4,1)S(1)}, s32[]{:S(2)}) async-start(s8[8388608]{0:T(1024)(128)(4,1)} %bitcast.36), calls=%async_computation.1 | async-start | bytes 8388608
  89.2 30.5 %copy-start.1 = (bf16[2,4,8,24,1024]{4,3,2,1,0:T(8,128)(2,1)S(1)}, bf16[2,4,8,24,1024]{4,3,2,1,0:T(8,128)(2,1)}, u32[]{:S(2)}) copy-start(bf16[2,4,8,24,1024]{4,3,2,1,0:T(8,128)(2,1)} %get-tuple-element.13) | copy-start | bytes 9437188

commit v2 on v1

v2 whole, which is shorter than its diff:
```python
import functools

import jax
import jax.numpy as jnp
from jax import lax
from jax.experimental import pallas as pl
from jax.experimental.pallas import tpu as pltpu
from jax.sharding import PartitionSpec as P

FF = 8192
LANES = 128
ROOT = 0.7978845608028654
CUBE = 0.044715
MESH = pl.DeviceIdType.MESH


def meet(peers):
    barrier = pltpu.get_barrier_semaphore()
    for peer in peers:
        pl.semaphore_signal(barrier, inc=1, device_id=peer, device_id_type=MESH)
    pl.semaphore_wait(barrier, len(peers))


def send(src, dst, send_sem, recv_sem, peer):
    copy = pltpu.make_async_remote_copy(
        src_ref=src,
        dst_ref=dst,
        send_sem=send_sem,
        recv_sem=recv_sem,
        device_id=peer,
        device_id_type=MESH,
    )
    copy.start()
    return copy


def layer_kernel(
    spans,
    tokens,
    out_grad,
    picks,
    gates,
    counts,
    weight_in,
    weight_out,
    slices,
    all_pre,
    all_hidden,
    rows_out,
    gates_out,
    tables,
    w1,
    w2,
    rows,
    scales,
    pre,
    back,
    gate,
    pre_grad,
    hidden,
    terms,
    beside_terms,
    pair_sum,
    line_terms,
    table_sem,
    w_sem,
    s_send,
    s_recv,
    g_send,
    g_recv,
    gx_send,
    gx_recv,
    dp_send,
    dp_recv,
    keep_sem,
    own_sem,
    a_send,
    a_recv,
    x_send,
    x_recv,
    z_send,
    z_recv,
):
    parts = all_pre.shape[0]
    count, slots, model_width = rows.shape[1:]
    row_count = count * slots
    lines = count // 2
    width = model_width // parts
    e = lax.axis_index("expert")
    d = lax.axis_index("dp")
    z = e // 2
    x = lax.rem(e, 2)
    after = lax.rem(e + 2, count)
    beside = e + 1 - 2 * x
    twin = d + 1 - 2 * lax.rem(d, 2)
    across = lax.rem(d + 2, parts)
    loads = [
        pltpu.make_async_copy(src, tables.at[i], table_sem.at[i])
        for i, src in enumerate((tokens, out_grad))
    ] + [
        pltpu.make_async_copy(src, dst, w_sem.at[i])
        for i, (src, dst) in enumerate(((weight_in, w1), (weight_out, w2)))
    ]
    for copy in loads:
        copy.start()
    group = [lax.rem(e + 2 * t, count) for t in range(1, lines)]
    group += [lax.rem(beside + 2 * t, count) for t in range(lines)]
    meet([(peer, d) for peer in group] + [(e, lax.rem(d + k, parts)) for k in range(1, parts)])
    sent = []

    def block(b, c):
        return rows.at[:, b, :, pl.ds(c * width, width)]

    def to_z(b, s, c):
        sent.append(send(block(b, c), block(b, c), g_send.at[s, c], g_recv.at[s, c], (after, d)))

    def to_beside(b, s, c):
        sent.append(send(block(b, c), block(b, c), gx_send.at[s, c], gx_recv.at[s, c], (beside, d)))

    def to_dp(b, c):
        @pl.when(d == c)
        def _():
            pltpu.make_async_copy(block(b, c), slices.at[:, d, b], keep_sem).start()

        @pl.when(d != c)
        def _():
            send(block(b, c), slices.at[:, d, b], dp_send, dp_recv.at[d], (e, c))

    def arrived(ref, sem):
        pltpu.make_async_copy(ref, ref, sem).wait()

    chosen = lax.broadcasted_iota(jnp.int32, (tables.shape[1], slots), 0) == picks[...]
    chosen = chosen.astype(jnp.float32).astype(jnp.bfloat16)
    for copy in loads[:2]:
        copy.wait()
    for c in range(parts):
        cols = slice(c * width, (c + 1) * width)
        for i in range(2):
            rows[i, e, :, cols] = lax.dot_general(
                chosen,
                tables[i, :, cols],
                (((0,), (0,)), ((), ())),
                preferred_element_type=jnp.float32,
            ).astype(jnp.bfloat16)
        to_beside(e, 0, c)
        to_z(e, 0, c)
        to_dp(e, c)
    slot = lax.broadcasted_iota(jnp.int32, (slots, slots), 1)
    live = slot == lax.broadcasted_iota(jnp.int32, (slots, slots), 0)
    live = jnp.logical_and(live, slot < counts[...])
    scale = jnp.where(live, jnp.broadcast_to(gates[...].astype(jnp.float32), (slots, slots)), 0.0)
    scale = jnp.sum(scale, axis=1, keepdims=True)
    scales[e] = jnp.broadcast_to(scale, (slots, LANES))
    for i, peer in enumerate(group):
        sent.append(send(scales.at[e], scales.at[e], s_send.at[i], s_recv.at[e], (peer, d)))

    def multiply(c):
        cols = slice(c * width, (c + 1) * width)
        for i, (weight, total) in enumerate(((w1, pre), (w2, back))):
            part = rows[i, :, :, cols].astype(jnp.float32).reshape(row_count, width)
            part = jnp.dot(
                part.astype(jnp.bfloat16), weight[cols, :], preferred_element_type=jnp.float32
            )
            if c == 0:
                total[...] = part
            else:
                total[...] += part

    for s in range(1, lines + 1):
        if s < lines:
            b = lax.rem(e + count - 2 * s, count)
            for c in range(parts):
                arrived(block(b, c), g_recv.at[s - 1, c])
                to_beside(b, s, c)
                if s < lines - 1:
                    to_z(b, s, c)
                to_dp(b, c)
        b = lax.rem(beside + count - 2 * (s - 1), count)
        for c in range(parts):
            arrived(block(b, c), gx_recv.at[s - 1, c])
            to_dp(b, c)
            if s == lines:
                if c == 0:
                    for copy in loads[2:]:
                        copy.wait()
                multiply(c)

    for peer in group:
        arrived(scales.at[peer], s_recv.at[peer])
    row_scale = scales[...].reshape(row_count, LANES)
    step = 32
    for start in range(0, row_count, step):
        here = slice(start, start + step)
        v, g, scale = pre[here, :], back[here, :], row_scale[here, :1]
        square = v * v
        bend = jnp.tanh(ROOT * v * (1.0 + CUBE * square))
        half = 0.5 * (1.0 + bend)
        value = v * half
        slope = half + 0.5 * v * (1.0 - bend * bend) * ROOT * (1.0 + 3.0 * CUBE * square)
        pre_grad[here, :] = (scale * g * slope).astype(jnp.bfloat16)
        hidden[here, :] = (scale * value).astype(jnp.bfloat16)
        gate[here, :] = jnp.broadcast_to(
            jnp.sum(value * g, axis=1, keepdims=True), (step, LANES)
        )

    pairs = ((pre_grad, all_pre), (hidden, all_hidden))
    for i, (src, dst) in enumerate(pairs):
        sent.append(send(src, dst.at[d], a_send.at[0, i], a_recv.at[0, i], (e, across)))
    for i, (src, dst) in enumerate(pairs):
        sent.append(send(src, dst.at[d], a_send.at[1, i], a_recv.at[1, i], (e, twin)))
        pltpu.make_async_copy(src, dst.at[d], own_sem.at[i]).start()

    def to_x(k, value):
        start, size = spans[k]
        cols = pl.ds(start, size)
        value = value.reshape(lines, 2, slots, size).astype(jnp.bfloat16)
        terms[0, :, :, start : start + size] = value[:, 0]
        terms[1, :, :, start : start + size] = value[:, 1]
        sent.append(
            send(
                terms.at[1 - x, :, :, cols],
                beside_terms.at[:, :, cols],
                x_send.at[k],
                x_recv.at[k],
                (beside, d),
            )
        )

    def to_lines(k):
        start, size = spans[k]
        cols = slice(start, start + size)
        here = pl.ds(start, size)
        arrived(beside_terms.at[:, :, here], x_recv.at[k])
        pair_sum[:, :, cols] = (
            terms[x, :, :, cols].astype(jnp.float32)
            + beside_terms[:, :, cols].astype(jnp.float32)
        ).astype(jnp.bfloat16)
        for t in range(1, lines):
            sent.append(
                send(
                    pair_sum.at[lax.rem(z + t, lines), :, here],
                    line_terms.at[t - 1, :, here],
                    z_send.at[t - 1, k],
                    z_recv.at[t - 1, k],
                    (lax.rem(e + 2 * t, count), d),
                )
            )

    to_x(0, gate[...])
    for k in range(1, len(spans)):
        start, size = spans[k]
        to_x(
            k,
            lax.dot_general(
                pre_grad[...],
                w1[start : start + size, :],
                (((1,), (1,)), ((), ())),
                preferred_element_type=jnp.float32,
            ),
        )
    for k in range(len(spans)):
        to_lines(k)
    for i, (_, dst) in enumerate(pairs):
        arrived(dst.at[across], a_recv.at[0, i])
        sent.append(
            send(dst.at[across], dst.at[across], a_send.at[2, i], a_recv.at[2, i], (e, twin))
        )
    for k, (start, size) in enumerate(spans):
        cols = slice(start, start + size)
        total = terms[x, z, :, cols].astype(jnp.float32)
        total += beside_terms[z, :, cols].astype(jnp.float32)
        for t in range(1, lines):
            arrived(line_terms.at[t - 1, :, pl.ds(start, size)], z_recv.at[t - 1, k])
            total += line_terms[t - 1, :, cols].astype(jnp.float32)
        if start < model_width:
            rows_out[:, cols] = total.astype(jnp.bfloat16)
        else:
            gates_out[...] = total
    for i, (src, dst) in enumerate(pairs):
        pltpu.make_async_copy(src, dst.at[d], own_sem.at[i]).wait()
        for hop, owner in ((1, twin), (2, lax.rem(twin + 2, parts))):
            arrived(dst.at[owner], a_recv.at[hop, i])
    for copy in sent:
        copy.wait_send()
    arrived(slices.at[:, pl.ds(0, parts - 1)], dp_send)
    arrived(slices.at[:, d], keep_sem)
    for k in range(1, parts):
        owner = lax.rem(d + k, parts)
        arrived(slices.at[:, owner], dp_recv.at[owner])


def layer(tokens, out_grad, picks, gates, counts, weight_in, weight_out, count, parts):
    t_dev, model_width = tokens.shape
    slots = picks.shape[-1]
    units = weight_in.shape[1]
    row_count = count * slots
    lines = count // 2
    width = model_width // parts
    spans = [(model_width, LANES)] + [(k * width, width) for k in range(parts)]
    wide = model_width + LANES
    dma = pltpu.SemaphoreType.DMA
    vmem = pl.BlockSpec(memory_space=pltpu.VMEM)
    anywhere = pl.BlockSpec(memory_space=pl.ANY)
    bf16, f32 = jnp.bfloat16, jnp.float32
    return pl.pallas_call(
        functools.partial(layer_kernel, spans),
        out_shape=(
            jax.ShapeDtypeStruct((2, parts, count, slots, width), bf16),
            jax.ShapeDtypeStruct((parts, row_count, units), bf16),
            jax.ShapeDtypeStruct((parts, row_count, units), bf16),
            jax.ShapeDtypeStruct((slots, model_width), bf16),
            jax.ShapeDtypeStruct((slots, LANES), f32),
        ),
        in_specs=[anywhere, anywhere, vmem, vmem, vmem, anywhere, anywhere],
        out_specs=[anywhere, anywhere, anywhere, vmem, vmem],
        scratch_shapes=[
            pltpu.VMEM((2, t_dev, model_width), bf16),
            pltpu.VMEM((model_width, units), bf16),
            pltpu.VMEM((model_width, units), bf16),
            pltpu.VMEM((2, count, slots, model_width), bf16),
            pltpu.VMEM((count, slots, LANES), f32),
            pltpu.VMEM((row_count, units), f32),
            pltpu.VMEM((row_count, units), f32),
            pltpu.VMEM((row_count, LANES), f32),
            pltpu.VMEM((row_count, units), bf16),
            pltpu.VMEM((row_count, units), bf16),
            pltpu.VMEM((2, lines, slots, wide), bf16),
            pltpu.VMEM((lines, slots, wide), bf16),
            pltpu.VMEM((lines, slots, wide), bf16),
            pltpu.VMEM((lines - 1, slots, wide), bf16),
            dma((2,)),
            dma((2,)),
            dma((count - 1,)),
            dma((count,)),
            dma((lines - 1, parts)),
            dma((lines - 1, parts)),
            dma((lines, parts)),
            dma((lines, parts)),
            dma,
            dma((parts,)),
            dma,
            dma((2,)),
            dma((3, 2)),
            dma((3, 2)),
            dma((len(spans),)),
            dma((len(spans),)),
            dma((lines - 1, len(spans))),
            dma((lines - 1, len(spans))),
        ],
        compiler_params=pltpu.CompilerParams(
            collective_id=0, has_side_effects=True, vmem_limit_bytes=56 << 20
        ),
        cost_estimate=pl.CostEstimate(
            flops=6 * row_count * units * model_width,
            bytes_accessed=32 << 20,
            transcendentals=0,
        ),
        name="layer",
    )(tokens, out_grad, picks, gates, counts, weight_in, weight_out)


def local(tokens, out_grad, gates, picks, counts, w_in, w_out):
    t_dev, model_width = tokens.shape
    slot_count = picks.shape[2]
    parts = lax.axis_size("dp")
    count = lax.axis_size("expert")
    row_count = count * slot_count
    slices, all_pre, all_hidden, summed_rows, summed_gates = layer(
        tokens, out_grad, picks[0], gates[0], counts, w_in[0], w_out[0], count, parts
    )

    def weight_grad(columns, units):
        return lax.dot_general(
            columns.reshape(parts * row_count, model_width // parts),
            units.reshape(parts * row_count, units.shape[-1]),
            (((0,), (0,)), ((), ())),
            preferred_element_type=jnp.float32,
        ).astype(jnp.bfloat16)[None]

    chosen = (picks[0, 0][:, None] == jnp.arange(t_dev)[None, :]).astype(jnp.bfloat16)
    tokens_grad = lax.dot_general(
        chosen, summed_rows, (((0,), (0,)), ((), ())), preferred_element_type=jnp.float32
    ).astype(jnp.bfloat16)
    live = jnp.arange(slot_count)[None, :] < counts[0][:, None]
    gates_grad = jnp.where(live, summed_gates[:, 0][None], 0.0)[None]
    return (
        tokens_grad,
        gates_grad,
        weight_grad(slices[0], all_pre),
        weight_grad(slices[1], all_hidden),
    )


def local_many(tokens, out_grad, gates, picks, counts, w_in, w_out):
    t_dev, model_width = tokens.shape
    expert_count = picks.shape[1]
    slot_count = picks.shape[2]
    part_units = w_in.shape[2]
    part_count = FF // part_units
    expert_devices = lax.axis_size("expert")
    row_index = picks[0].reshape(-1)
    live = jnp.arange(slot_count)[None, :] < counts[0][:, None]
    scale = jnp.where(live, gates[0], jnp.zeros_like(gates[0]))

    def exchange(values):
        return lax.all_to_all(values, "expert", split_axis=0, concat_axis=0, tiled=True)

    def spread(values):
        wide = jnp.broadcast_to(values[:, None], (expert_count, part_count) + values.shape[1:])
        return exchange(wide.reshape((expert_devices,) + values.shape[1:]))

    row_count = expert_devices * slot_count
    picked_shape = (expert_count, slot_count, model_width)
    rows_x = spread(tokens[row_index].reshape(picked_shape)).reshape(row_count, model_width)
    rows_dy = spread(out_grad[row_index].reshape(picked_shape)).reshape(row_count, model_width)
    row_scale = spread(scale).reshape(row_count, 1).astype(jnp.float32)
    weight_in, weight_out = w_in[0], w_out[0]
    pre = jnp.dot(rows_x, weight_in, preferred_element_type=jnp.float32)
    back = jnp.dot(rows_dy, weight_out, preferred_element_type=jnp.float32)
    hidden, gelu_back = jax.vjp(jax.nn.gelu, pre)
    gate_part = jnp.sum(hidden * back, axis=-1)
    pre_grad = gelu_back(row_scale * back)[0].astype(jnp.bfloat16)
    scaled_hidden = (row_scale * hidden).astype(jnp.bfloat16)
    row_part = lax.dot_general(
        pre_grad, weight_in, (((1,), (1,)), ((), ())), preferred_element_type=jnp.float32
    )

    def weight_grad(columns, units):
        columns = lax.all_to_all(columns, "dp", split_axis=1, concat_axis=0, tiled=True)
        units = lax.all_gather(units, "dp", axis=0, tiled=True)
        return lax.dot_general(
            columns, units, (((0,), (0,)), ((), ())), preferred_element_type=jnp.float32
        ).astype(jnp.bfloat16)[None]

    back_shape = (expert_devices, slot_count, model_width)
    back_rows = exchange(row_part.reshape(back_shape).astype(jnp.bfloat16)).astype(jnp.float32)
    back_gates = exchange(gate_part.reshape(back_shape[:2]))
    summed_rows = jnp.sum(back_rows.reshape((expert_count, part_count) + back_shape[1:]), axis=1)
    summed_gates = jnp.sum(back_gates.reshape(expert_count, part_count, slot_count), axis=1)
    empty_rows = jnp.zeros((t_dev, model_width), jnp.float32)
    tokens_grad = (
        empty_rows.at[row_index].add(summed_rows.reshape(-1, model_width)).astype(jnp.bfloat16)
    )
    gates_grad = jnp.where(live, summed_gates, jnp.zeros_like(summed_gates))[None]
    return (
        tokens_grad,
        gates_grad,
        weight_grad(rows_x, pre_grad),
        weight_grad(rows_dy, scaled_hidden),
    )


def solution(mesh):
    placed = (
        P(("expert", "dp"), None),
        P(("expert", "dp"), None),
        P(("expert", "dp"), None, None),
        P(("expert", "dp"), None, None),
        P(("expert", "dp"), None),
        P("expert", None, None),
        P("expert", None, None),
    )

    def run(*arrays):
        one = arrays[3].shape[1] == 1 and mesh.shape["dp"] == 4
        return jax.shard_map(
            local if one else local_many,
            mesh=mesh,
            in_specs=placed,
            out_specs=(
                P(("expert", "dp"), None),
                P(("expert", "dp"), None, None),
                P("expert", "dp", None),
                P("expert", "dp", None),
            ),
            check_vma=False,
        )(*arrays)

    return run
```

time: 130 us -> 89.7 us (0.69)
  blocking collectives: 23.1 us -> 0 us
  matrix products: 22.7 us -> 9.75 us
  Pallas kernels: 76.2 us -> 74.7 us
    unnamed x1 -> x0, blocking collectives: 23.1 us -> none
    dot_general x4 -> x0, matrix products: 13 us -> none  [the longest x1 5.37 us: local(): jnp.dot(rows[0].reshape(row_count, model_width), weight_in, preferred_ele...]
    slice x1 -> x0, local copies, waits for them, and re-layouts: 2.38 us -> none  [local(): rows[1].reshape(row_count, model_width)]
    slice x1, local copies, waits for them, and re-layouts: 0.37 us -> 2.34 us  [local(): slices[1]]
    pallas_call x2 -> x1, Pallas kernels: 76.2 us -> 74.7 us  [layer(): pl.pallas_call(functools.partial(layer_kernel, spans), out_shape=(jax.Sha...]
    unnamed x17 -> x8, local copies, waits for them, and re-layouts: 1.5 us -> 0.02 us
where the time goes in v2:
time: 89.7 us; the launch traced here: 89.4 us
  Pallas kernels  74.7 us (83%)
  matrix products  9.75 us (11%)
  local copies, waits for them, and re-layouts  3.18 us (4%)
  between operations  1.31 us (1%)
    pallas_call x1, Pallas kernels, layer(): pl.pallas_call(functools.partial(layer_kernel, spans), out_shape=(jax.Sha...  74.7 us
    dot_general x2, matrix products, weight_grad(): lax.dot_general(columns.reshape(parts * row_count, model_width // parts),...  6.36 us
    dot_general x1, matrix products, local(): lax.dot_general(chosen, summed_rows, (((0,), (0,)), ((), ())), preferred_...  3.39 us
    slice x1, local copies, waits for them, and re-layouts, local(): slices[1]  2.34 us

profile of v2, /device:TPU:0, one launch (start us, length us, event | category | flops | bytes accessed | tf_op | source)
XLA Modules:
  0.0 89.4 jit_solution(5745756779853360033)
XLA Ops:
  1.3 74.7 %layer.1 = (bf16[2,4,8,24,1024]{4,3,2,1,0:T(8,128)(2,1)}, bf16[4,192,1024]{2,1,0:T(8,128)(2,1)}, bf16[4,192,1024]{2,1,0:T(8,128)(2,1)}, bf16[24,4096]{1,0:T(8,128)(2,1)}, f32[24,128]{1,0:T(8,128)}) custom-call(bf16[512,4096]{1,0:T(8,128)(2,1)} %tokens.1, bf16[512,4096]{1,0:T(8,128)(2,1)} %out_grad.1, s32[1,24]{1,0:T(1,128)} %bitcast.26, ...), custom_call_target="tpu_custom_call" | custom-call | flops 4831838208 | bytes 33554432 | tf_op jit(solution)/shard_map/layer/pallas_call | solution.py:305
  76.0 0.8 slice_reduce_fusion
  76.8 0.5 compare_select_fusion
  77.3 0.0 copy-start.3
  77.3 2.3 %fusion.1 = (bf16[1,4,8,24,1024]{4,3,2,1,0:T(8,128)(2,1)S(1)}, bf16[1,4,8,24,1024]{4,3,2,1,0:T(8,128)(2,1)S(1)}) fusion(bf16[2,4,8,24,1024]{4,3,2,1,0:T(8,128)(2,1)} %get-tuple-element.11), kind=kLoop, calls=%fused_computation.7 | loop fusion | bytes 6291456 | tf_op jit(solution)/shard_map/slice | solution.py:390
  79.7 0.0 copy-done.3
  79.7 0.0 copy-start.2
  79.7 3.2 %convert_bitcast_fusion = bf16[1,1024,1024]{2,1,0:T(8,128)(2,1)} fusion(bf16[768,1024]{1,0:T(8,128)(2,1)S(1)} %bitcast.25, bf16[768,1024]{1,0:T(8,128)(2,1)S(1)} %bitcast.30), kind=kOutput, calls=%fused_computation.1 | convolution fusion | flops 1611661312 | bytes 5242880 | tf_op jit(solution)/shard_map/dot_general | solution.py:373
  82.9 0.0 copy-done.2
  82.9 0.0 copy-start
  82.9 0.0 copy-start.1
  82.9 3.2 %convert_bitcast_fusion.1 = bf16[1,1024,1024]{2,1,0:T(8,128)(2,1)} fusion(bf16[768,1024]{1,0:T(8,128)(2,1)S(1)} %bitcast.24, bf16[768,1024]{1,0:T(8,128)(2,1)S(1)} %bitcast.29), kind=kOutput, calls=%fused_computation.2 | convolution fusion | flops 1611661312 | bytes 5242880 | tf_op jit(solution)/shard_map/dot_general | solution.py:373
  86.0 0.0 copy-done
  86.0 0.0 copy-done.1
  86.0 3.4 %convolution_convert_fusion = bf16[512,4096]{1,0:T(8,128)(2,1)} fusion(bf16[24,4096]{1,0:T(8,128)(2,1)S(1)} %copy-done, s32[24]{0:T(128)S(1)} %bitcast.27), kind=kOutput, calls=%fused_computation | convolution fusion | flops 102772736 | bytes 4391008 | tf_op jit(solution)/shard_map/dot_general | solution.py:381
Async XLA Ops:
  77.3 2.4 %copy-start.3 = (bf16[4,192,1024]{2,1,0:T(8,128)(2,1)S(1)}, bf16[4,192,1024]{2,1,0:T(8,128)(2,1)}, u32[]{:S(2)}) copy-start(bf16[4,192,1024]{2,1,0:T(8,128)(2,1)} %get-tuple-element.13) | copy-start | bytes 4718596
  79.7 3.2 %copy-start.2 = (bf16[4,192,1024]{2,1,0:T(8,128)(2,1)S(1)}, bf16[4,192,1024]{2,1,0:T(8,128)(2,1)}, u32[]{:S(2)}) copy-start(bf16[4,192,1024]{2,1,0:T(8,128)(2,1)} %get-tuple-element.12) | copy-start | bytes 4718596
  82.9 3.2 %copy-start = (bf16[24,4096]{1,0:T(8,128)(2,1)S(1)}, bf16[24,4096]{1,0:T(8,128)(2,1)}, u32[]{:S(2)}) copy-start(bf16[24,4096]{1,0:T(8,128)(2,1)} %get-tuple-element.9) | copy-start | bytes 589828
  82.9 3.2 %copy-start.1 = (s32[1,1,24]{2,1,0:T(1,128)S(1)}, s32[1,1,24]{2,1,0:T(1,128)}, u32[]{:S(2)}) copy-start(s32[1,1,24]{2,1,0:T(1,128)} %param.10) | copy-start | bytes 292

commit v3 on v2

--- a/solution.py
+++ b/solution.py
@@ -82,9 +82,9 @@
     z_recv,
 ):
     parts = all_pre.shape[0]
-    count, slots, model_width = rows.shape[1:]
-    row_count = count * slots
-    lines = count // 2
+    lines, _, slots, model_width = rows.shape[1:]
+    count = 2 * lines
+    pair_rows = 2 * slots
     width = model_width // parts
     e = lax.axis_index("expert")
     d = lax.axis_index("dp")
@@ -108,23 +108,30 @@
     meet([(peer, d) for peer in group] + [(e, lax.rem(d + k, parts)) for k in range(1, parts)])
     sent = []
 
-    def block(b, c):
-        return rows.at[:, b, :, pl.ds(c * width, width)]
-
-    def to_z(b, s, c):
-        sent.append(send(block(b, c), block(b, c), g_send.at[s, c], g_recv.at[s, c], (after, d)))
-
-    def to_beside(b, s, c):
-        sent.append(send(block(b, c), block(b, c), gx_send.at[s, c], gx_recv.at[s, c], (beside, d)))
-
-    def to_dp(b, c):
+    def line(s):
+        return lax.rem(z + lines - s, lines)
+
+    def block(zz, xx, c):
+        return rows.at[:, zz, xx, :, pl.ds(c * width, width)]
+
+    def to_z(s, c):
+        ref = block(line(s), x, c)
+        sent.append(send(ref, ref, g_send.at[s, c], g_recv.at[s, c], (after, d)))
+
+    def to_beside(s, c):
+        ref = block(line(s), x, c)
+        sent.append(send(ref, ref, gx_send.at[s, c], gx_recv.at[s, c], (beside, d)))
+
+    def to_dp(s, xx, c):
+        ref = block(line(s), xx, c)
+
         @pl.when(d == c)
         def _():
-            pltpu.make_async_copy(block(b, c), slices.at[:, d, b], keep_sem).start()
+            pltpu.make_async_copy(ref, slices.at[:, d, line(s), xx], keep_sem).start()
 
         @pl.when(d != c)
         def _():
-            send(block(b, c), slices.at[:, d, b], dp_send, dp_recv.at[d], (e, c))
+            send(ref, slices.at[:, d, line(s), xx], dp_send, dp_recv.at[d], (e, c))
 
     def arrived(ref, sem):
         pltpu.make_async_copy(ref, ref, sem).wait()
@@ -136,15 +143,15 @@
     for c in range(parts):
         cols = slice(c * width, (c + 1) * width)
         for i in range(2):
-            rows[i, e, :, cols] = lax.dot_general(
+            rows[i, z, x, :, cols] = lax.dot_general(
                 chosen,
                 tables[i, :, cols],
                 (((0,), (0,)), ((), ())),
                 preferred_element_type=jnp.float32,
             ).astype(jnp.bfloat16)
-        to_beside(e, 0, c)
-        to_z(e, 0, c)
-        to_dp(e, c)
+        to_beside(0, c)
+        to_z(0, c)
+        to_dp(0, x, c)
     slot = lax.broadcasted_iota(jnp.int32, (slots, slots), 1)
     live = slot == lax.broadcasted_iota(jnp.int32, (slots, slots), 0)
     live = jnp.logical_and(live, slot < counts[...])
@@ -154,132 +161,139 @@
     for i, peer in enumerate(group):
         sent.append(send(scales.at[e], scales.at[e], s_send.at[i], s_recv.at[e], (peer, d)))
 
-    def multiply(c):
-        cols = slice(c * width, (c + 1) * width)
-        for i, (weight, total) in enumerate(((w1, pre), (w2, back))):
-            part = rows[i, :, :, cols].astype(jnp.float32).reshape(row_count, width)
-            part = jnp.dot(
-                part.astype(jnp.bfloat16), weight[cols, :], preferred_element_type=jnp.float32
+    pairs = ((pre_grad, all_pre), (hidden, all_hidden))
+
+    def forward(s):
+        for c in range(parts):
+            arrived(block(line(s), x, c), g_recv.at[s - 1, c])
+            if s < lines - 1:
+                to_z(s, c)
+            to_beside(s, c)
+            to_dp(s, x, c)
+
+    def multiply(s):
+        for c in range(parts):
+            arrived(block(line(s), 1 - x, c), gx_recv.at[s, c])
+            to_dp(s, 1 - x, c)
+            if s == 0 and c == 0:
+                for copy in loads[2:]:
+                    copy.wait()
+            cols = slice(c * width, (c + 1) * width)
+            for i, (weight, total) in enumerate(((w1, pre), (w2, back))):
+                part = rows[i, line(s), :, :, cols].astype(jnp.float32).reshape(pair_rows, width)
+                part = jnp.dot(
+                    part.astype(jnp.bfloat16), weight[cols, :], preferred_element_type=jnp.float32
+                )
+                if c == 0:
+                    total[...] = part
+                else:
+                    total[...] += part
+
+    def activate(s):
+        zz = line(s)
+        for owner in (2 * zz + x, 2 * zz + 1 - x)[s == 0 :]:
+            arrived(scales.at[owner], s_recv.at[owner])
+        row_scale = scales[pl.ds(2 * zz, 2)].reshape(pair_rows, LANES)
+        step = 16
+        for start in range(0, pair_rows, step):
+            here = slice(start, start + step)
+            v, g, scale = pre[here, :], back[here, :], row_scale[here, :1]
+            square = v * v
+            bend = jnp.tanh(ROOT * v * (1.0 + CUBE * square))
+            half = 0.5 * (1.0 + bend)
+            value = v * half
+            slope = half + 0.5 * v * (1.0 - bend * bend) * ROOT * (1.0 + 3.0 * CUBE * square)
+            pre_grad[zz, here, :] = (scale * g * slope).astype(jnp.bfloat16)
+            hidden[zz, here, :] = (scale * value).astype(jnp.bfloat16)
+            gate[here, :] = jnp.broadcast_to(
+                jnp.sum(value * g, axis=1, keepdims=True), (step, LANES)
             )
-            if c == 0:
-                total[...] = part
-            else:
-                total[...] += part
-
-    for s in range(1, lines + 1):
-        if s < lines:
-            b = lax.rem(e + count - 2 * s, count)
-            for c in range(parts):
-                arrived(block(b, c), g_recv.at[s - 1, c])
-                to_beside(b, s, c)
-                if s < lines - 1:
-                    to_z(b, s, c)
-                to_dp(b, c)
-        b = lax.rem(beside + count - 2 * (s - 1), count)
+        for i, (src, dst) in enumerate(pairs):
+            for hop, peer in ((0, across), (1, twin)):
+                sems = a_send.at[hop, s, i], a_recv.at[hop, s, i]
+                sent.append(send(src.at[zz], dst.at[d, zz], *sems, (e, peer)))
+
+    def pass_on(s):
+        for i, (_, dst) in enumerate(pairs):
+            ref = dst.at[across, line(s)]
+            arrived(ref, a_recv.at[0, s, i])
+            sent.append(send(ref, ref, a_send.at[2, s, i], a_recv.at[2, s, i], (e, twin)))
+
+    def give_back(s):
+        zz = line(s)
+        value = gate[...].reshape(2, slots, LANES).astype(jnp.bfloat16)
+        terms[zz, :, :, model_width:] = value
         for c in range(parts):
-            arrived(block(b, c), gx_recv.at[s - 1, c])
-            to_dp(b, c)
-            if s == lines:
-                if c == 0:
-                    for copy in loads[2:]:
-                        copy.wait()
-                multiply(c)
-
-    for peer in group:
-        arrived(scales.at[peer], s_recv.at[peer])
-    row_scale = scales[...].reshape(row_count, LANES)
-    step = 32
-    for start in range(0, row_count, step):
-        here = slice(start, start + step)
-        v, g, scale = pre[here, :], back[here, :], row_scale[here, :1]
-        square = v * v
-        bend = jnp.tanh(ROOT * v * (1.0 + CUBE * square))
-        half = 0.5 * (1.0 + bend)
-        value = v * half
-        slope = half + 0.5 * v * (1.0 - bend * bend) * ROOT * (1.0 + 3.0 * CUBE * square)
-        pre_grad[here, :] = (scale * g * slope).astype(jnp.bfloat16)
-        hidden[here, :] = (scale * value).astype(jnp.bfloat16)
-        gate[here, :] = jnp.broadcast_to(
-            jnp.sum(value * g, axis=1, keepdims=True), (step, LANES)
-        )
-
-    pairs = ((pre_grad, all_pre), (hidden, all_hidden))
-    for i, (src, dst) in enumerate(pairs):
-        sent.append(send(src, dst.at[d], a_send.at[0, i], a_recv.at[0, i], (e, across)))
-    for i, (src, dst) in enumerate(pairs):
-        sent.append(send(src, dst.at[d], a_send.at[1, i], a_recv.at[1, i], (e, twin)))
-        pltpu.make_async_copy(src, dst.at[d], own_sem.at[i]).start()
-
-    def to_x(k, value):
-        start, size = spans[k]
-        cols = pl.ds(start, size)
-        value = value.reshape(lines, 2, slots, size).astype(jnp.bfloat16)
-        terms[0, :, :, start : start + size] = value[:, 0]
-        terms[1, :, :, start : start + size] = value[:, 1]
-        sent.append(
-            send(
-                terms.at[1 - x, :, :, cols],
-                beside_terms.at[:, :, cols],
-                x_send.at[k],
-                x_recv.at[k],
-                (beside, d),
-            )
-        )
-
-    def to_lines(k):
-        start, size = spans[k]
-        cols = slice(start, start + size)
-        here = pl.ds(start, size)
-        arrived(beside_terms.at[:, :, here], x_recv.at[k])
-        pair_sum[:, :, cols] = (
-            terms[x, :, :, cols].astype(jnp.float32)
-            + beside_terms[:, :, cols].astype(jnp.float32)
-        ).astype(jnp.bfloat16)
-        for t in range(1, lines):
-            sent.append(
-                send(
-                    pair_sum.at[lax.rem(z + t, lines), :, here],
-                    line_terms.at[t - 1, :, here],
-                    z_send.at[t - 1, k],
-                    z_recv.at[t - 1, k],
-                    (lax.rem(e + 2 * t, count), d),
-                )
-            )
-
-    to_x(0, gate[...])
-    for k in range(1, len(spans)):
-        start, size = spans[k]
-        to_x(
-            k,
-            lax.dot_general(
-                pre_grad[...],
-                w1[start : start + size, :],
+            cols = slice(c * width, (c + 1) * width)
+            value = lax.dot_general(
+                pre_grad[zz],
+                w1[cols, :],
                 (((1,), (1,)), ((), ())),
                 preferred_element_type=jnp.float32,
-            ),
-        )
-    for k in range(len(spans)):
-        to_lines(k)
-    for i, (_, dst) in enumerate(pairs):
-        arrived(dst.at[across], a_recv.at[0, i])
-        sent.append(
-            send(dst.at[across], dst.at[across], a_send.at[2, i], a_recv.at[2, i], (e, twin))
-        )
+            )
+            terms[zz, :, :, cols] = value.reshape(2, slots, width).astype(jnp.bfloat16)
+            for k, (start, size) in enumerate(spans):
+                if (c + 1) * width == min(start + size, model_width):
+                    here = pl.ds(start, size)
+                    sent.append(
+                        send(
+                            terms.at[zz, 1 - x, :, here],
+                            beside_terms.at[zz, :, here],
+                            x_send.at[s, k],
+                            x_recv.at[s, k],
+                            (beside, d),
+                        )
+                    )
+
+    def to_line(s):
+        zz = line(s)
+        for k, (start, size) in enumerate(spans):
+            cols = slice(start, start + size)
+            here = pl.ds(start, size)
+            arrived(beside_terms.at[zz, :, here], x_recv.at[s, k])
+            if s > 0:
+                total = terms[zz, x, :, cols].astype(jnp.float32)
+                total += beside_terms[zz, :, cols].astype(jnp.float32)
+                pair_sum[s - 1, :, cols] = total.astype(jnp.bfloat16)
+                sent.append(
+                    send(
+                        pair_sum.at[s - 1, :, here],
+                        line_terms.at[s - 1, :, here],
+                        z_send.at[s - 1, k],
+                        z_recv.at[s - 1, k],
+                        (2 * zz + x, d),
+                    )
+                )
+
+    for s in range(lines):
+        if s < lines - 1:
+            forward(s + 1)
+        multiply(s)
+        activate(s)
+        give_back(s)
+        if s > 0:
+            to_line(s - 1)
+            pass_on(s - 1)
+    for i, (src, dst) in enumerate(pairs):
+        pltpu.make_async_copy(src, dst.at[d], own_sem.at[i]).start()
+    to_line(lines - 1)
+    pass_on(lines - 1)
     for k, (start, size) in enumerate(spans):
         cols = slice(start, start + size)
-        total = terms[x, z, :, cols].astype(jnp.float32)
+        total = terms[z, x, :, cols].astype(jnp.float32)
         total += beside_terms[z, :, cols].astype(jnp.float32)
-        for t in range(1, lines):
-            arrived(line_terms.at[t - 1, :, pl.ds(start, size)], z_recv.at[t - 1, k])
-            total += line_terms[t - 1, :, cols].astype(jnp.float32)
-        if start < model_width:
-            rows_out[:, cols] = total.astype(jnp.bfloat16)
-        else:
-            gates_out[...] = total
+        for s in range(1, lines):
+            arrived(line_terms.at[s - 1, :, pl.ds(start, size)], z_recv.at[s - 1, k])
+            total += line_terms[s - 1, :, cols].astype(jnp.float32)
+        inside = min(size, model_width - start)
+        rows_out[:, start : start + inside] = total[:, :inside].astype(jnp.bfloat16)
+        if inside < size:
+            gates_out[...] = total[:, inside:]
     for i, (src, dst) in enumerate(pairs):
         pltpu.make_async_copy(src, dst.at[d], own_sem.at[i]).wait()
         for hop, owner in ((1, twin), (2, lax.rem(twin + 2, parts))):
-            arrived(dst.at[owner], a_recv.at[hop, i])
+            for s in range(lines):
+                arrived(dst.at[owner, line(s)], a_recv.at[hop, s, i])
     for copy in sent:
         copy.wait_send()
     arrived(slices.at[:, pl.ds(0, parts - 1)], dp_send)
@@ -296,8 +310,10 @@
     row_count = count * slots
     lines = count // 2
     width = model_width // parts
-    spans = [(model_width, LANES)] + [(k * width, width) for k in range(parts)]
     wide = model_width + LANES
+    half = model_width // 2
+    spans = [(0, half), (half, wide - half)]
+    pair_rows = 2 * slots
     dma = pltpu.SemaphoreType.DMA
     vmem = pl.BlockSpec(memory_space=pltpu.VMEM)
     anywhere = pl.BlockSpec(memory_space=pl.ANY)
@@ -305,9 +321,9 @@
     return pl.pallas_call(
         functools.partial(layer_kernel, spans),
         out_shape=(
-            jax.ShapeDtypeStruct((2, parts, count, slots, width), bf16),
-            jax.ShapeDtypeStruct((parts, row_count, units), bf16),
-            jax.ShapeDtypeStruct((parts, row_count, units), bf16),
+            jax.ShapeDtypeStruct((2, parts, lines, 2, slots, width), bf16),
+            jax.ShapeDtypeStruct((parts, lines, pair_rows, units), bf16),
+            jax.ShapeDtypeStruct((parts, lines, pair_rows, units), bf16),
             jax.ShapeDtypeStruct((slots, model_width), bf16),
             jax.ShapeDtypeStruct((slots, LANES), f32),
         ),
@@ -317,16 +333,16 @@
             pltpu.VMEM((2, t_dev, model_width), bf16),
             pltpu.VMEM((model_width, units), bf16),
             pltpu.VMEM((model_width, units), bf16),
-            pltpu.VMEM((2, count, slots, model_width), bf16),
+            pltpu.VMEM((2, lines, 2, slots, model_width), bf16),
             pltpu.VMEM((count, slots, LANES), f32),
-            pltpu.VMEM((row_count, units), f32),
-            pltpu.VMEM((row_count, units), f32),
-            pltpu.VMEM((row_count, LANES), f32),
-            pltpu.VMEM((row_count, units), bf16),
-            pltpu.VMEM((row_count, units), bf16),
-            pltpu.VMEM((2, lines, slots, wide), bf16),
+            pltpu.VMEM((pair_rows, units), f32),
+            pltpu.VMEM((pair_rows, units), f32),
+            pltpu.VMEM((pair_rows, LANES), f32),
+            pltpu.VMEM((lines, pair_rows, units), bf16),
+            pltpu.VMEM((lines, pair_rows, units), bf16),
+            pltpu.VMEM((lines, 2, slots, wide), bf16),
             pltpu.VMEM((lines, slots, wide), bf16),
-            pltpu.VMEM((lines, slots, wide), bf16),
+            pltpu.VMEM((lines - 1, slots, wide), bf16),
             pltpu.VMEM((lines - 1, slots, wide), bf16),
             dma((2,)),
             dma((2,)),
@@ -340,10 +356,10 @@
             dma((parts,)),
             dma,
             dma((2,)),
-            dma((3, 2)),
-            dma((3, 2)),
-            dma((len(spans),)),
-            dma((len(spans),)),
+            dma((3, lines, 2)),
+            dma((3, lines, 2)),
+            dma((lines, len(spans))),
+            dma((lines, len(spans))),
             dma((lines - 1, len(spans))),
             dma((lines - 1, len(spans))),
         ],

time: 89.7 us -> 91.2 us (1.017)
  Pallas kernels: 74.7 us -> 76.1 us
    pallas_call x1, Pallas kernels: 74.7 us -> 76.1 us  [layer(): pl.pallas_call(functools.partial(layer_kernel, spans), out_shape=(jax.Sha...]
where the time goes in v3:
time: 91.2 us; the launch traced here: 90.9 us
  Pallas kernels  76.1 us (83%)
  matrix products  9.75 us (11%)
  local copies, waits for them, and re-layouts  3.22 us (4%)
  between operations  1.32 us (1%)
    pallas_call x1, Pallas kernels, layer(): pl.pallas_call(functools.partial(layer_kernel, spans), out_shape=(jax.Sha...  76.1 us
    dot_general x2, matrix products, weight_grad(): lax.dot_general(columns.reshape(parts * row_count, model_width // parts),...  6.36 us
    dot_general x1, matrix products, local(): lax.dot_general(chosen, summed_rows, (((0,), (0,)), ((), ())), preferred_...  3.39 us
    slice x1, local copies, waits for them, and re-layouts, local(): slices[1]  2.39 us

profile of v3, /device:TPU:0, one launch (start us, length us, event | category | flops | bytes accessed | tf_op | source)
XLA Modules:
  0.0 90.9 jit_solution(3446961422930402988)
XLA Ops:
  1.3 76.1 %layer.1 = (bf16[2,4,4,2,24,1024]{5,4,3,2,1,0:T(8,128)(2,1)}, bf16[4,4,48,1024]{3,2,1,0:T(8,128)(2,1)}, bf16[4,4,48,1024]{3,2,1,0:T(8,128)(2,1)}, bf16[24,4096]{1,0:T(8,128)(2,1)}, f32[24,128]{1,0:T(8,128)}) custom-call(bf16[512,4096]{1,0:T(8,128)(2,1)} %tokens.1, bf16[512,4096]{1,0:T(8,128)(2,1)} %out_grad.1, s32[1,24]{1,0:T(1,128)} %bitcast.26, ...), custom_call_target="tpu_custom_call" | custom-call | flops 4831838208 | bytes 33554432 | tf_op jit(solution)/shard_map/layer/pallas_call | solution.py:321
  77.4 0.8 slice_reduce_fusion
  78.2 0.5 compare_select_fusion
  78.8 0.0 copy-start.3
  78.8 2.4 %fusion.1 = (bf16[1,4,4,2,24,1024]{5,4,3,2,1,0:T(8,128)(2,1)S(1)}, bf16[1,4,4,2,24,1024]{5,4,3,2,1,0:T(8,128)(2,1)S(1)}) fusion(bf16[2,4,4,2,24,1024]{5,4,3,2,1,0:T(8,128)(2,1)} %get-tuple-element.11), kind=kLoop, calls=%fused_computation.7 | loop fusion | bytes 6291456 | tf_op jit(solution)/shard_map/slice | solution.py:406
  81.2 0.0 copy-done.3
  81.2 0.0 copy-start.2
  81.2 3.2 %convert_bitcast_fusion = bf16[1,1024,1024]{2,1,0:T(8,128)(2,1)} fusion(bf16[768,1024]{1,0:T(8,128)(2,1)S(1)} %bitcast.25, bf16[768,1024]{1,0:T(8,128)(2,1)S(1)} %bitcast.30), kind=kOutput, calls=%fused_computation.1 | convolution fusion | flops 1611661312 | bytes 5242880 | tf_op jit(solution)/shard_map/dot_general | solution.py:389
  84.4 0.0 copy-done.2
  84.4 0.0 copy-start
  84.4 0.0 copy-start.1
  84.4 3.2 %convert_bitcast_fusion.1 = bf16[1,1024,1024]{2,1,0:T(8,128)(2,1)} fusion(bf16[768,1024]{1,0:T(8,128)(2,1)S(1)} %bitcast.24, bf16[768,1024]{1,0:T(8,128)(2,1)S(1)} %bitcast.29), kind=kOutput, calls=%fused_computation.2 | convolution fusion | flops 1611661312 | bytes 5242880 | tf_op jit(solution)/shard_map/dot_general | solution.py:389
  87.5 0.0 copy-done
  87.5 0.0 copy-done.1
  87.5 3.4 %convolution_convert_fusion = bf16[512,4096]{1,0:T(8,128)(2,1)} fusion(bf16[24,4096]{1,0:T(8,128)(2,1)S(1)} %copy-done, s32[24]{0:T(128)S(1)} %bitcast.27), kind=kOutput, calls=%fused_computation | convolution fusion | flops 102772736 | bytes 4391008 | tf_op jit(solution)/shard_map/dot_general | solution.py:397
Async XLA Ops:
  78.8 2.4 %copy-start.3 = (bf16[4,4,48,1024]{3,2,1,0:T(8,128)(2,1)S(1)}, bf16[4,4,48,1024]{3,2,1,0:T(8,128)(2,1)}, u32[]{:S(2)}) copy-start(bf16[4,4,48,1024]{3,2,1,0:T(8,128)(2,1)} %get-tuple-element.13) | copy-start | bytes 4718596
  81.2 3.2 %copy-start.2 = (bf16[4,4,48,1024]{3,2,1,0:T(8,128)(2,1)S(1)}, bf16[4,4,48,1024]{3,2,1,0:T(8,128)(2,1)}, u32[]{:S(2)}) copy-start(bf16[4,4,48,1024]{3,2,1,0:T(8,128)(2,1)} %get-tuple-element.12) | copy-start | bytes 4718596
  84.4 3.2 %copy-start = (bf16[24,4096]{1,0:T(8,128)(2,1)S(1)}, bf16[24,4096]{1,0:T(8,128)(2,1)}, u32[]{:S(2)}) copy-start(bf16[24,4096]{1,0:T(8,128)(2,1)} %get-tuple-element.9) | copy-start | bytes 589828
  84.4 3.2 %copy-start.1 = (s32[1,1,24]{2,1,0:T(1,128)S(1)}, s32[1,1,24]{2,1,0:T(1,128)}, u32[]{:S(2)}) copy-start(s32[1,1,24]{2,1,0:T(1,128)} %param.10) | copy-start | bytes 292

commit v4 on v3

--- a/solution.py
+++ b/solution.py
@@ -43,7 +43,8 @@
     counts,
     weight_in,
     weight_out,
-    slices,
+    x_slices,
+    dy_slices,
     all_pre,
     all_hidden,
     rows_out,
@@ -122,16 +123,20 @@
         ref = block(line(s), x, c)
         sent.append(send(ref, ref, gx_send.at[s, c], gx_recv.at[s, c], (beside, d)))
 
-    def to_dp(s, xx, c):
-        ref = block(line(s), xx, c)
-
-        @pl.when(d == c)
-        def _():
-            pltpu.make_async_copy(ref, slices.at[:, d, line(s), xx], keep_sem).start()
-
-        @pl.when(d != c)
-        def _():
-            send(ref, slices.at[:, d, line(s), xx], dp_send, dp_recv.at[d], (e, c))
+    def to_dp(s, pick):
+        for c in range(parts):
+            for i, slices in enumerate((x_slices, dy_slices)):
+                ref = rows.at[i, line(s), pick, :, pl.ds(c * width, width)]
+
+                @pl.when(d == c)
+                def _():
+                    mine = slices.at[d, line(s), pick]
+                    pltpu.make_async_copy(ref, mine, keep_sem.at[i]).start()
+
+                @pl.when(d != c)
+                def _():
+                    there = slices.at[d, line(s), pick]
+                    send(ref, there, dp_send.at[i], dp_recv.at[i, d], (e, c))
 
     def arrived(ref, sem):
         pltpu.make_async_copy(ref, ref, sem).wait()
@@ -151,7 +156,7 @@
             ).astype(jnp.bfloat16)
         to_beside(0, c)
         to_z(0, c)
-        to_dp(0, x, c)
+    to_dp(0, x)
     slot = lax.broadcasted_iota(jnp.int32, (slots, slots), 1)
     live = slot == lax.broadcasted_iota(jnp.int32, (slots, slots), 0)
     live = jnp.logical_and(live, slot < counts[...])
@@ -169,18 +174,25 @@
             if s < lines - 1:
                 to_z(s, c)
             to_beside(s, c)
-            to_dp(s, x, c)
-
-    def multiply(s):
+
+    def collect(s, pick):
         for c in range(parts):
             arrived(block(line(s), 1 - x, c), gx_recv.at[s, c])
-            to_dp(s, 1 - x, c)
-            if s == 0 and c == 0:
-                for copy in loads[2:]:
-                    copy.wait()
+        to_dp(s, pick)
+
+    def multiply(group):
+        if group[0] == 0:
+            for copy in loads[2:]:
+                copy.wait()
+        for c in range(parts):
             cols = slice(c * width, (c + 1) * width)
             for i, (weight, total) in enumerate(((w1, pre), (w2, back))):
-                part = rows[i, line(s), :, :, cols].astype(jnp.float32).reshape(pair_rows, width)
+                part = jnp.concatenate(
+                    [
+                        rows[i, line(s), :, :, cols].astype(jnp.float32).reshape(pair_rows, width)
+                        for s in group
+                    ]
+                )
                 part = jnp.dot(
                     part.astype(jnp.bfloat16), weight[cols, :], preferred_element_type=jnp.float32
                 )
@@ -189,29 +201,31 @@
                 else:
                     total[...] += part
 
-    def activate(s):
-        zz = line(s)
-        for owner in (2 * zz + x, 2 * zz + 1 - x)[s == 0 :]:
-            arrived(scales.at[owner], s_recv.at[owner])
-        row_scale = scales[pl.ds(2 * zz, 2)].reshape(pair_rows, LANES)
-        step = 16
-        for start in range(0, pair_rows, step):
-            here = slice(start, start + step)
-            v, g, scale = pre[here, :], back[here, :], row_scale[here, :1]
-            square = v * v
-            bend = jnp.tanh(ROOT * v * (1.0 + CUBE * square))
-            half = 0.5 * (1.0 + bend)
-            value = v * half
-            slope = half + 0.5 * v * (1.0 - bend * bend) * ROOT * (1.0 + 3.0 * CUBE * square)
-            pre_grad[zz, here, :] = (scale * g * slope).astype(jnp.bfloat16)
-            hidden[zz, here, :] = (scale * value).astype(jnp.bfloat16)
-            gate[here, :] = jnp.broadcast_to(
-                jnp.sum(value * g, axis=1, keepdims=True), (step, LANES)
-            )
-        for i, (src, dst) in enumerate(pairs):
-            for hop, peer in ((0, across), (1, twin)):
-                sems = a_send.at[hop, s, i], a_recv.at[hop, s, i]
-                sent.append(send(src.at[zz], dst.at[d, zz], *sems, (e, peer)))
+    def activate(group):
+        for j, s in enumerate(group):
+            zz = line(s)
+            for owner in (2 * zz + x, 2 * zz + 1 - x)[s == 0 :]:
+                arrived(scales.at[owner], s_recv.at[owner])
+            row_scale = scales[pl.ds(2 * zz, 2)].reshape(pair_rows, LANES)
+            step = 16
+            for start in range(0, pair_rows, step):
+                here = slice(start, start + step)
+                there = slice(j * pair_rows + start, j * pair_rows + start + step)
+                v, g, scale = pre[there, :], back[there, :], row_scale[here, :1]
+                square = v * v
+                bend = jnp.tanh(ROOT * v * (1.0 + CUBE * square))
+                half = 0.5 * (1.0 + bend)
+                value = v * half
+                slope = half + 0.5 * v * (1.0 - bend * bend) * ROOT * (1.0 + 3.0 * CUBE * square)
+                pre_grad[zz, here, :] = (scale * g * slope).astype(jnp.bfloat16)
+                hidden[zz, here, :] = (scale * value).astype(jnp.bfloat16)
+                gate[there, :] = jnp.broadcast_to(
+                    jnp.sum(value * g, axis=1, keepdims=True), (step, LANES)
+                )
+            for i, (src, dst) in enumerate(pairs):
+                for hop, peer in ((0, across), (1, twin)):
+                    sems = a_send.at[hop, s, i], a_recv.at[hop, s, i]
+                    sent.append(send(src.at[zz], dst.at[d, zz], *sems, (e, peer)))
 
     def pass_on(s):
         for i, (_, dst) in enumerate(pairs):
@@ -219,65 +233,86 @@
             arrived(ref, a_recv.at[0, s, i])
             sent.append(send(ref, ref, a_send.at[2, s, i], a_recv.at[2, s, i], (e, twin)))
 
-    def give_back(s):
-        zz = line(s)
-        value = gate[...].reshape(2, slots, LANES).astype(jnp.bfloat16)
-        terms[zz, :, :, model_width:] = value
-        for c in range(parts):
-            cols = slice(c * width, (c + 1) * width)
+    def give_back(group):
+        units = jnp.concatenate([pre_grad[line(s)] for s in group])
+
+        def keep(cols, value):
+            size = value.shape[-1]
+            value = value.reshape(len(group), 2, slots, size).astype(jnp.bfloat16)
+            for j, s in enumerate(group):
+                terms[line(s), :, :, cols] = value[j]
+
+        keep(slice(model_width, model_width + LANES), gate[...])
+        for k, (start, size) in enumerate(spans):
+            cols = slice(start, start + width)
             value = lax.dot_general(
-                pre_grad[zz],
-                w1[cols, :],
-                (((1,), (1,)), ((), ())),
-                preferred_element_type=jnp.float32,
+                units, w1[cols, :], (((1,), (1,)), ((), ())), preferred_element_type=jnp.float32
             )
-            terms[zz, :, :, cols] = value.reshape(2, slots, width).astype(jnp.bfloat16)
-            for k, (start, size) in enumerate(spans):
-                if (c + 1) * width == min(start + size, model_width):
-                    here = pl.ds(start, size)
-                    sent.append(
-                        send(
-                            terms.at[zz, 1 - x, :, here],
-                            beside_terms.at[zz, :, here],
-                            x_send.at[s, k],
-                            x_recv.at[s, k],
-                            (beside, d),
-                        )
-                    )
-
-    def to_line(s):
-        zz = line(s)
-        for k, (start, size) in enumerate(spans):
-            cols = slice(start, start + size)
+            keep(cols, value)
             here = pl.ds(start, size)
-            arrived(beside_terms.at[zz, :, here], x_recv.at[s, k])
-            if s > 0:
-                total = terms[zz, x, :, cols].astype(jnp.float32)
-                total += beside_terms[zz, :, cols].astype(jnp.float32)
-                pair_sum[s - 1, :, cols] = total.astype(jnp.bfloat16)
+            for s in group:
                 sent.append(
                     send(
-                        pair_sum.at[s - 1, :, here],
-                        line_terms.at[s - 1, :, here],
-                        z_send.at[s - 1, k],
-                        z_recv.at[s - 1, k],
-                        (2 * zz + x, d),
+                        terms.at[line(s), 1 - x, :, here],
+                        beside_terms.at[line(s), :, here],
+                        x_send.at[s, k],
+                        x_recv.at[s, k],
+                        (beside, d),
                     )
                 )
 
-    for s in range(lines):
-        if s < lines - 1:
+    def to_line(s, k):
+        zz = line(s)
+        start, size = spans[k]
+        cols = slice(start, start + size)
+        here = pl.ds(start, size)
+        arrived(beside_terms.at[zz, :, here], x_recv.at[s, k])
+        if s > 0:
+            total = terms[zz, x, :, cols].astype(jnp.float32)
+            total += beside_terms[zz, :, cols].astype(jnp.float32)
+            pair_sum[s - 1, :, cols] = total.astype(jnp.bfloat16)
+            sent.append(
+                send(
+                    pair_sum.at[s - 1, :, here],
+                    line_terms.at[s - 1, :, here],
+                    z_send.at[s - 1, k],
+                    z_recv.at[s - 1, k],
+                    (2 * zz + x, d),
+                )
+            )
+
+    early, late = range(lines // 2), range(lines // 2, lines)
+    for s in early:
+        if s > 0:
+            forward(s)
+            to_dp(s, x)
+    for s in early:
+        if s == early[-1]:
             forward(s + 1)
-        multiply(s)
-        activate(s)
-        give_back(s)
-        if s > 0:
-            to_line(s - 1)
-            pass_on(s - 1)
+        collect(s, 1 - x)
+    multiply(early)
+    activate(early)
+    for s in late:
+        if s > late[0]:
+            forward(s)
+    give_back(early)
+    for s in late:
+        collect(s, slice(None))
+    multiply(late)
+    activate(late)
+    for s in early:
+        for k in range(len(spans)):
+            to_line(s, k)
+    give_back(late)
     for i, (src, dst) in enumerate(pairs):
         pltpu.make_async_copy(src, dst.at[d], own_sem.at[i]).start()
-    to_line(lines - 1)
-    pass_on(lines - 1)
+    for s in early:
+        pass_on(s)
+    for k in range(len(spans)):
+        for s in late:
+            to_line(s, k)
+    for s in late:
+        pass_on(s)
     for k, (start, size) in enumerate(spans):
         cols = slice(start, start + size)
         total = terms[z, x, :, cols].astype(jnp.float32)
@@ -288,7 +323,11 @@
         inside = min(size, model_width - start)
         rows_out[:, start : start + inside] = total[:, :inside].astype(jnp.bfloat16)
         if inside < size:
-            gates_out[...] = total[:, inside:]
+            own = jnp.logical_and(
+                slot == lax.broadcasted_iota(jnp.int32, (slots, slots), 0), slot < counts[...]
+            )
+            total = jnp.where(own, total[:, inside : inside + 1], 0.0)
+            gates_out[...] = jnp.sum(total, axis=0, keepdims=True)
     for i, (src, dst) in enumerate(pairs):
         pltpu.make_async_copy(src, dst.at[d], own_sem.at[i]).wait()
         for hop, owner in ((1, twin), (2, lax.rem(twin + 2, parts))):
@@ -296,11 +335,12 @@
                 arrived(dst.at[owner, line(s)], a_recv.at[hop, s, i])
     for copy in sent:
         copy.wait_send()
-    arrived(slices.at[:, pl.ds(0, parts - 1)], dp_send)
-    arrived(slices.at[:, d], keep_sem)
-    for k in range(1, parts):
-        owner = lax.rem(d + k, parts)
-        arrived(slices.at[:, owner], dp_recv.at[owner])
+    for i, slices in enumerate((x_slices, dy_slices)):
+        arrived(slices.at[pl.ds(0, parts - 1)], dp_send.at[i])
+        arrived(slices.at[d], keep_sem.at[i])
+        for k in range(1, parts):
+            owner = lax.rem(d + k, parts)
+            arrived(slices.at[owner], dp_recv.at[i, owner])
 
 
 def layer(tokens, out_grad, picks, gates, counts, weight_in, weight_out, count, parts):
@@ -311,8 +351,8 @@
     lines = count // 2
     width = model_width // parts
     wide = model_width + LANES
-    half = model_width // 2
-    spans = [(0, half), (half, wide - half)]
+    spans = [(k * width, width) for k in range(parts - 1)]
+    spans.append((model_width - width, width + LANES))
     pair_rows = 2 * slots
     dma = pltpu.SemaphoreType.DMA
     vmem = pl.BlockSpec(memory_space=pltpu.VMEM)
@@ -321,23 +361,24 @@
     return pl.pallas_call(
         functools.partial(layer_kernel, spans),
         out_shape=(
-            jax.ShapeDtypeStruct((2, parts, lines, 2, slots, width), bf16),
+            jax.ShapeDtypeStruct((parts, lines, 2, slots, width), bf16),
+            jax.ShapeDtypeStruct((parts, lines, 2, slots, width), bf16),
             jax.ShapeDtypeStruct((parts, lines, pair_rows, units), bf16),
             jax.ShapeDtypeStruct((parts, lines, pair_rows, units), bf16),
             jax.ShapeDtypeStruct((slots, model_width), bf16),
-            jax.ShapeDtypeStruct((slots, LANES), f32),
+            jax.ShapeDtypeStruct((1, slots), f32),
         ),
         in_specs=[anywhere, anywhere, vmem, vmem, vmem, anywhere, anywhere],
-        out_specs=[anywhere, anywhere, anywhere, vmem, vmem],
+        out_specs=[anywhere, anywhere, anywhere, anywhere, vmem, vmem],
         scratch_shapes=[
             pltpu.VMEM((2, t_dev, model_width), bf16),
             pltpu.VMEM((model_width, units), bf16),
             pltpu.VMEM((model_width, units), bf16),
             pltpu.VMEM((2, lines, 2, slots, model_width), bf16),
             pltpu.VMEM((count, slots, LANES), f32),
-            pltpu.VMEM((pair_rows, units), f32),
-            pltpu.VMEM((pair_rows, units), f32),
-            pltpu.VMEM((pair_rows, LANES), f32),
+            pltpu.VMEM((row_count // 2, units), f32),
+            pltpu.VMEM((row_count // 2, units), f32),
+            pltpu.VMEM((row_count // 2, LANES), f32),
             pltpu.VMEM((lines, pair_rows, units), bf16),
             pltpu.VMEM((lines, pair_rows, units), bf16),
             pltpu.VMEM((lines, 2, slots, wide), bf16),
@@ -352,9 +393,9 @@
             dma((lines - 1, parts)),
             dma((lines, parts)),
             dma((lines, parts)),
-            dma,
-            dma((parts,)),
-            dma,
+            dma((2,)),
+            dma((2, parts)),
+            dma((2,)),
             dma((2,)),
             dma((3, lines, 2)),
             dma((3, lines, 2)),
@@ -381,7 +422,7 @@
     parts = lax.axis_size("dp")
     count = lax.axis_size("expert")
     row_count = count * slot_count
-    slices, all_pre, all_hidden, summed_rows, summed_gates = layer(
+    x_slices, dy_slices, all_pre, all_hidden, summed_rows, gates_grad = layer(
         tokens, out_grad, picks[0], gates[0], counts, w_in[0], w_out[0], count, parts
     )
 
@@ -397,13 +438,11 @@
     tokens_grad = lax.dot_general(
         chosen, summed_rows, (((0,), (0,)), ((), ())), preferred_element_type=jnp.float32
     ).astype(jnp.bfloat16)
-    live = jnp.arange(slot_count)[None, :] < counts[0][:, None]
-    gates_grad = jnp.where(live, summed_gates[:, 0][None], 0.0)[None]
     return (
         tokens_grad,
-        gates_grad,
-        weight_grad(slices[0], all_pre),
-        weight_grad(slices[1], all_hidden),
+        gates_grad[None],
+        weight_grad(x_slices, all_pre),
+        weight_grad(dy_slices, all_hidden),
     )
 
 

time: 91.2 us -> 90.2 us (0.989)
  local copies, waits for them, and re-layouts: 3.22 us -> 0.53 us
  matrix products: 9.75 us -> 12 us
    slice x2 -> x0, local copies, waits for them, and re-layouts: 3.21 us -> none  [the longest x1 2.39 us: local(): slices[1]]
    dot_general x2, matrix products: 6.36 us -> 8.57 us  [weight_grad(): lax.dot_general(columns.reshape(parts * row_count, model_width // parts),...]
where the time goes in v4:
time: 90.2 us; the launch traced here: 90.1 us
  Pallas kernels  76.2 us (84%)
  matrix products  12 us (13%)
  between operations  1.32 us (1%)
    pallas_call x1, Pallas kernels, layer(): pl.pallas_call(functools.partial(layer_kernel, spans), out_shape=(jax.Sha...  76.2 us
    dot_general x2, matrix products, weight_grad(): lax.dot_general(columns.reshape(parts * row_count, model_width // parts),...  8.57 us
    dot_general x1, matrix products, local(): lax.dot_general(chosen, summed_rows, (((0,), (0,)), ((), ())), preferred_...  3.39 us

profile of v4, /device:TPU:0, one launch (start us, length us, event | category | flops | bytes accessed | tf_op | source)
XLA Modules:
  0.0 90.1 jit_solution(7845168192734938162)
XLA Ops:
  1.3 76.2 %layer.1 = (bf16[4,4,2,24,1024]{4,3,2,1,0:T(8,128)(2,1)}, bf16[4,4,2,24,1024]{4,3,2,1,0:T(8,128)(2,1)}, bf16[4,4,48,1024]{3,2,1,0:T(8,128)(2,1)}, bf16[4,4,48,10...) custom-call(bf16[512,4096]{1,0:T(8,128)(2,1)} %tokens.1, bf16[512,4096]{1,0:T(8,128)(2,1)} %out_grad.1, ...), custom_call_target="tpu_custom_call" | custom-call | flops 4831838208 | bytes 33554432 | tf_op jit(solution)/shard_map/layer/pallas_call | solution.py:361
  77.5 0.0 copy-start.2
  77.5 0.0 copy-start.3
  77.5 5.4 %convert_bitcast_fusion.1 = bf16[1,1024,1024]{2,1,0:T(8,128)(2,1)} fusion(bf16[768,1024]{1,0:T(8,128)(2,1)} %bitcast.26, bf16[768,1024]{1,0:T(8,128)(2,1)} %bitcast.27), kind=kOutput, calls=%fused_computation.2 | convolution fusion | flops 1611661312 | bytes 5242880 | tf_op jit(solution)/shard_map/dot_general | solution.py:430
  82.9 0.0 copy-done.2
  82.9 0.0 copy-done.3
  82.9 0.0 copy-start
  82.9 0.0 copy-start.1
  83.0 3.2 %convert_bitcast_fusion = bf16[1,1024,1024]{2,1,0:T(8,128)(2,1)} fusion(bf16[768,1024]{1,0:T(8,128)(2,1)S(1)} %bitcast.24, bf16[768,1024]{1,0:T(8,128)(2,1)S(1)} %bitcast.25), kind=kOutput, calls=%fused_computation.1 | convolution fusion | flops 1611661312 | bytes 5242880 | tf_op jit(solution)/shard_map/dot_general | solution.py:430
  86.1 0.0 copy-done
  86.1 0.0 copy-done.1
  86.1 0.0 copy-start.4
  86.1 3.4 %convolution_convert_fusion = bf16[512,4096]{1,0:T(8,128)(2,1)} fusion(bf16[24,4096]{1,0:T(8,128)(2,1)S(1)} %copy-done, s32[24]{0:T(128)S(1)} %bitcast.22), kind=kOutput, calls=%fused_computation | convolution fusion | flops 102772736 | bytes 4391008 | tf_op jit(solution)/shard_map/dot_general | solution.py:438
  89.5 0.0 copy-done.4
  89.5 0.5 copy.13
Async XLA Ops:
  77.5 5.4 %copy-start.2 = (bf16[4,4,2,24,1024]{4,3,2,1,0:T(8,128)(2,1)S(1)}, bf16[4,4,2,24,1024]{4,3,2,1,0:T(8,128)(2,1)}, u32[]{:S(2)}) copy-start(bf16[4,4,2,24,1024]{4,3,2,1,0:T(8,128)(2,1)} %get-tuple-element.14) | copy-start | bytes 4718596
  77.5 5.4 %copy-start.3 = (bf16[4,4,48,1024]{3,2,1,0:T(8,128)(2,1)S(1)}, bf16[4,4,48,1024]{3,2,1,0:T(8,128)(2,1)}, u32[]{:S(2)}) copy-start(bf16[4,4,48,1024]{3,2,1,0:T(8,128)(2,1)} %get-tuple-element.15) | copy-start | bytes 4718596
  82.9 3.2 %copy-start = (bf16[24,4096]{1,0:T(8,128)(2,1)S(1)}, bf16[24,4096]{1,0:T(8,128)(2,1)}, u32[]{:S(2)}) copy-start(bf16[24,4096]{1,0:T(8,128)(2,1)} %get-tuple-element.10) | copy-start | bytes 589828
  82.9 3.2 %copy-start.1 = (s32[1,1,24]{2,1,0:T(1,128)S(1)}, s32[1,1,24]{2,1,0:T(1,128)}, u32[]{:S(2)}) copy-start(s32[1,1,24]{2,1,0:T(1,128)} %param.10) | copy-start | bytes 292
  86.1 3.4 %copy-start.4 = (f32[1,24]{1,0:T(1,128)S(1)}, f32[1,24]{1,0:T(1,128)}, u32[]{:S(2)}) copy-start(f32[1,24]{1,0:T(1,128)} %get-tuple-element.11) | copy-start | bytes 292

commit v5 on v2

--- a/solution.py
+++ b/solution.py
@@ -275,7 +275,10 @@
         if start < model_width:
             rows_out[:, cols] = total.astype(jnp.bfloat16)
         else:
-            gates_out[...] = total
+            own = slot == lax.broadcasted_iota(jnp.int32, (slots, slots), 0)
+            own = jnp.logical_and(own, slot < counts[...])
+            total = jnp.where(own, total[:, :1], 0.0)
+            gates_out[...] = jnp.sum(total, axis=0, keepdims=True)
     for i, (src, dst) in enumerate(pairs):
         pltpu.make_async_copy(src, dst.at[d], own_sem.at[i]).wait()
         for hop, owner in ((1, twin), (2, lax.rem(twin + 2, parts))):
@@ -309,7 +312,7 @@
             jax.ShapeDtypeStruct((parts, row_count, units), bf16),
             jax.ShapeDtypeStruct((parts, row_count, units), bf16),
             jax.ShapeDtypeStruct((slots, model_width), bf16),
-            jax.ShapeDtypeStruct((slots, LANES), f32),
+            jax.ShapeDtypeStruct((1, slots), f32),
         ),
         in_specs=[anywhere, anywhere, vmem, vmem, vmem, anywhere, anywhere],
         out_specs=[anywhere, anywhere, anywhere, vmem, vmem],
@@ -365,7 +368,7 @@
     parts = lax.axis_size("dp")
     count = lax.axis_size("expert")
     row_count = count * slot_count
-    slices, all_pre, all_hidden, summed_rows, summed_gates = layer(
+    slices, all_pre, all_hidden, summed_rows, gates_grad = layer(
         tokens, out_grad, picks[0], gates[0], counts, w_in[0], w_out[0], count, parts
     )
 
@@ -381,11 +384,9 @@
     tokens_grad = lax.dot_general(
         chosen, summed_rows, (((0,), (0,)), ((), ())), preferred_element_type=jnp.float32
     ).astype(jnp.bfloat16)
-    live = jnp.arange(slot_count)[None, :] < counts[0][:, None]
-    gates_grad = jnp.where(live, summed_gates[:, 0][None], 0.0)[None]
     return (
         tokens_grad,
-        gates_grad,
+        gates_grad[None],
         weight_grad(slices[0], all_pre),
         weight_grad(slices[1], all_hidden),
     )

time: 89.7 us -> 88.8 us (0.990)
  no operation moved by 1% of the time
where the time goes in v5:
time: 88.8 us; the launch traced here: 88.6 us
  Pallas kernels  74.7 us (84%)
  matrix products  9.75 us (11%)
  local copies, waits for them, and re-layouts  2.87 us (3%)
  between operations  1.32 us (1%)
    pallas_call x1, Pallas kernels, layer(): pl.pallas_call(functools.partial(layer_kernel, spans), out_shape=(jax.Sha...  74.7 us
    dot_general x2, matrix products, weight_grad(): lax.dot_general(columns.reshape(parts * row_count, model_width // parts),...  6.36 us
    dot_general x1, matrix products, local(): lax.dot_general(chosen, summed_rows, (((0,), (0,)), ((), ())), preferred_...  3.39 us
    slice x1, local copies, waits for them, and re-layouts, local(): slices[1]  2.34 us

profile of v5, /device:TPU:0, one launch (start us, length us, event | category | flops | bytes accessed | tf_op | source)
XLA Modules:
  0.0 88.6 jit_solution(3423522541923022789)
XLA Ops:
  1.3 74.7 %layer.1 = (bf16[2,4,8,24,1024]{4,3,2,1,0:T(8,128)(2,1)}, bf16[4,192,1024]{2,1,0:T(8,128)(2,1)}, bf16[4,192,1024]{2,1,0:T(8,128)(2,1)}, bf16[24,4096]{1,0:T(8,128)(2,1)}, f32[1,24]{1,0:T(1,128)}) custom-call(bf16[512,4096]{1,0:T(8,128)(2,1)} %tokens.1, bf16[512,4096]{1,0:T(8,128)(2,1)} %out_grad.1, s32[1,24]{1,0:T(1,128)} %bitcast.23, ...), custom_call_target="tpu_custom_call" | custom-call | flops 4831838208 | bytes 33554432 | tf_op jit(solution)/shard_map/layer/pallas_call | solution.py:308
  75.9 0.0 copy-start.3
  76.0 2.3 %fusion.1 = (bf16[1,4,8,24,1024]{4,3,2,1,0:T(8,128)(2,1)S(1)}, bf16[1,4,8,24,1024]{4,3,2,1,0:T(8,128)(2,1)S(1)}) fusion(bf16[2,4,8,24,1024]{4,3,2,1,0:T(8,128)(2,1)} %get-tuple-element.11), kind=kLoop, calls=%fused_computation.5 | loop fusion | bytes 6291456 | tf_op jit(solution)/shard_map/slice | solution.py:391
  78.3 0.0 copy-done.3
  78.3 0.0 copy-start.2
  78.3 3.2 %convert_bitcast_fusion = bf16[1,1024,1024]{2,1,0:T(8,128)(2,1)} fusion(bf16[768,1024]{1,0:T(8,128)(2,1)S(1)} %bitcast.22, bf16[768,1024]{1,0:T(8,128)(2,1)S(1)} %bitcast.27), kind=kOutput, calls=%fused_computation.1 | convolution fusion | flops 1611661312 | bytes 5242880 | tf_op jit(solution)/shard_map/dot_general | solution.py:376
  81.5 0.0 copy-done.2
  81.5 0.0 copy-start
  81.5 0.0 copy-start.1
  81.5 3.2 %convert_bitcast_fusion.1 = bf16[1,1024,1024]{2,1,0:T(8,128)(2,1)} fusion(bf16[768,1024]{1,0:T(8,128)(2,1)S(1)} %bitcast.21, bf16[768,1024]{1,0:T(8,128)(2,1)S(1)} %bitcast.26), kind=kOutput, calls=%fused_computation.2 | convolution fusion | flops 1611661312 | bytes 5242880 | tf_op jit(solution)/shard_map/dot_general | solution.py:376
  84.7 0.0 copy-done
  84.7 0.0 copy-done.1
  84.7 0.0 copy-start.4
  84.7 3.4 %convolution_convert_fusion = bf16[512,4096]{1,0:T(8,128)(2,1)} fusion(bf16[24,4096]{1,0:T(8,128)(2,1)S(1)} %copy-done, s32[24]{0:T(128)S(1)} %bitcast.24), kind=kOutput, calls=%fused_computation | convolution fusion | flops 102772736 | bytes 4391008 | tf_op jit(solution)/shard_map/dot_general | solution.py:384
  88.1 0.0 copy-done.4
  88.1 0.5 copy.13
Async XLA Ops:
  75.9 2.4 %copy-start.3 = (bf16[4,192,1024]{2,1,0:T(8,128)(2,1)S(1)}, bf16[4,192,1024]{2,1,0:T(8,128)(2,1)}, u32[]{:S(2)}) copy-start(bf16[4,192,1024]{2,1,0:T(8,128)(2,1)} %get-tuple-element.13) | copy-start | bytes 4718596
  78.3 3.2 %copy-start.2 = (bf16[4,192,1024]{2,1,0:T(8,128)(2,1)S(1)}, bf16[4,192,1024]{2,1,0:T(8,128)(2,1)}, u32[]{:S(2)}) copy-start(bf16[4,192,1024]{2,1,0:T(8,128)(2,1)} %get-tuple-element.12) | copy-start | bytes 4718596
  81.5 3.2 %copy-start = (bf16[24,4096]{1,0:T(8,128)(2,1)S(1)}, bf16[24,4096]{1,0:T(8,128)(2,1)}, u32[]{:S(2)}) copy-start(bf16[24,4096]{1,0:T(8,128)(2,1)} %get-tuple-element.9) | copy-start | bytes 589828
  81.5 3.2 %copy-start.1 = (s32[1,1,24]{2,1,0:T(1,128)S(1)}, s32[1,1,24]{2,1,0:T(1,128)}, u32[]{:S(2)}) copy-start(s32[1,1,24]{2,1,0:T(1,128)} %param.10) | copy-start | bytes 292
  84.7 3.4 %copy-start.4 = (f32[1,24]{1,0:T(1,128)S(1)}, f32[1,24]{1,0:T(1,128)}, u32[]{:S(2)}) copy-start(f32[1,24]{1,0:T(1,128)} %get-tuple-element.10) | copy-start | bytes 292
